TPU v7x, 32 devices: a whole 2x2x4 slice. The times are simulated.
32 devices in a mesh: dp: 16 (over z, y, core), dir: 2 (over x).
Axes of the slice: x: 2, y: 2, z: 4, core: 2. Of those that a mesh axis runs over, the one named last changes fastest.
Arguments:
- tokens: bfloat16 [8192, 768], P(('dp', 'dir')), may hold values from -6 to 6
- layernorm_gain: float32 [768], replicated, may hold values from 0.5 to 1.5
- layernorm_bias: float32 [768], replicated, may hold values from -3 to 3
- up_weight: bfloat16 [768, 3072], replicated, may hold values from -0.21875 to 0.21875
- up_bias: float32 [3072], replicated, may hold values from -3 to 3
- value_weight: bfloat16 [768, 1536], replicated, may hold values from -0.21875 to 0.21875
- value_bias: float32 [1536], replicated, may hold values from -3 to 3
- step_log: float32 [1536], replicated, may hold values from -4.6 to -2.3
- decay_log: float32 [1536, 64], replicated, may hold values from -1 to 1
- frequency: float32 [1536, 64], replicated, may hold values from 0 to 50
- coef_real: float32 [1536, 64], replicated, may hold values from -3 to 3
- coef_imag: float32 [1536, 64], replicated, may hold values from -3 to 3
- skip_gain: float32 [1536], replicated, may hold values from -4 to 4
- gate_weight: bfloat16 [3072, 1536], replicated, may hold values from -0.109375 to 0.109375
- gate_bias: float32 [1536], replicated, may hold values from -3 to 3
- out_weight: bfloat16 [1536, 768], replicated, may hold values from -0.15625 to 0.15625
- out_bias: float32 [768], replicated, may hold values from -3 to 3
- cotangent: bfloat16 [8192, 768], P(('dp', 'dir')), may hold values from -6 to 6
Outputs:
- mixed: bfloat16 [8192, 768], P(('dp', 'dir'))
- grad_tokens: bfloat16 [8192, 768], P(('dp', 'dir'))
- grad_norm_gain: float32 [768], replicated
- grad_norm_bias: float32 [768], replicated
- grad_up_weight: float32 [768, 3072], P(('dp', 'dir'))
- grad_up_bias: float32 [3072], P(('dp', 'dir'))
- grad_value_weight: float32 [768, 1536], P(('dp', 'dir'))
- grad_value_bias: float32 [1536], P(('dp', 'dir'))
- grad_step_log: float32 [1536], P(('dp', 'dir'))
- grad_decay_log: float32 [1536, 64], P(('dp', 'dir'))
- grad_frequency: float32 [1536, 64], P(('dp', 'dir'))
- grad_coef_real: float32 [1536, 64], P(('dp', 'dir'))
- grad_coef_imag: float32 [1536, 64], P(('dp', 'dir'))
- grad_skip_gain: float32 [1536], P(('dp', 'dir'))
- grad_gate_weight: float32 [3072, 1536], P(('dp', 'dir'))
- grad_gate_bias: float32 [1536], P(('dp', 'dir'))
- grad_out_weight: float32 [1536, 768], P(('dp', 'dir'))
- grad_out_bias: float32 [768], replicated
All inputs are finite; a program needn't handle non-finite values.
Results may differ from a plain program's by a relative error of at most 0.0082.
Values may be sent and summed in bfloat16 or wider, within the bound.
No kernel may reach another device: no remote copies, remote signals or barrier semaphores. Data moves between devices by JAX's collectives and lax.ppermute only.
A program may use at most 256 MiB of HBM per device.

v0:
```python
import jax
import jax.numpy as jnp
from jax import lax
from jax.sharding import PartitionSpec as P

SEQ_LEN = 128


eps = 1e-05
root_half = 0.7071067811865476
inv_root_two_pi = 0.3989422804014327


def gelu_slope(v):
    return 0.5 * (1.0 + lax.erf(v * root_half)) + v * inv_root_two_pi * jnp.exp(-0.5 * v * v)


def kernel_rows(step_log, decay_log, frequency, coef_real, coef_imag, length):
    delta = jnp.exp(step_log)[:, None, None]
    lags = jnp.arange(length).astype(jnp.float32)[None, None, :]
    rate = jnp.exp(decay_log)[:, :, None]
    phase = frequency[:, :, None] * delta * lags
    damp = jnp.exp(-rate * delta * lags)
    terms = damp * (coef_real[:, :, None] * jnp.cos(phase) - coef_imag[:, :, None] * jnp.sin(phase))
    return delta[:, :, 0] * jnp.sum(terms, axis=1)


def toeplitz(kern, flip):
    length = kern.shape[1]
    rows_idx = jnp.arange(length)[:, None]
    cols_idx = jnp.arange(length)[None, :]
    gap = rows_idx - cols_idx
    table = jnp.take(kern, jnp.clip(gap, 0, length - 1), axis=1)
    table = jnp.where(gap[None] >= 0, table, jnp.zeros_like(table))
    return jnp.where(flip, jnp.swapaxes(table, 1, 2), table)


def apply_table(table_low, skip_part, flat):
    mixed = jnp.einsum("cts,nsc->ntc", table_low, flat, preferred_element_type=jnp.float32)
    return (mixed + skip_part * flat.astype(jnp.float32)).astype(jnp.bfloat16)


def apply_transpose(table_low, skip_part, flat):
    back = jnp.einsum("cts,ntc->nsc", table_low, flat, preferred_element_type=jnp.float32)
    return (back + skip_part * flat.astype(jnp.float32)).astype(jnp.bfloat16)


def local(
    tokens,
    layernorm_gain,
    layernorm_bias,
    up_weight,
    up_bias,
    value_weight,
    value_bias,
    step_log,
    decay_log,
    frequency,
    coef_real,
    coef_imag,
    skip_gain,
    gate_weight,
    gate_bias,
    out_weight,
    out_bias,
    cotangent,
):
    rows, width = tokens.shape
    chans = value_weight.shape[1]
    hidden_width = up_weight.shape[1]
    half = chans // 2
    length = SEQ_LEN
    seqs = rows // length
    inputs = tokens.astype(jnp.float32)
    feature_average = jnp.mean(inputs, axis=1, keepdims=True)
    centered_input = inputs - feature_average
    inverse_deviation = lax.rsqrt(
        jnp.mean(centered_input * centered_input, axis=1, keepdims=True) + eps
    )
    standardized_input = centered_input * inverse_deviation
    normalized_input = (standardized_input * layernorm_gain + layernorm_bias).astype(jnp.bfloat16)
    up_pre = jnp.dot(normalized_input, up_weight, preferred_element_type=jnp.float32) + up_bias
    up_act = jax.nn.gelu(up_pre, approximate=False).astype(jnp.bfloat16)
    value_pre = (
        jnp.dot(normalized_input, value_weight, preferred_element_type=jnp.float32) + value_bias
    )
    value_act = jax.nn.gelu(value_pre, approximate=False).astype(jnp.bfloat16)
    ssm_params = (step_log, decay_log, frequency, coef_real, coef_imag)
    value_seq = value_act.reshape(seqs, length, chans)
    side = lax.axis_index("dir")

    def local_table(params):
        pieces = [lax.dynamic_slice_in_dim(p, side * half, half, 0) for p in params]
        return toeplitz(kernel_rows(*pieces, length), side == 1)

    table, table_back = jax.vjp(local_table, ssm_params)
    table_low = table.astype(jnp.bfloat16)
    skip_part = lax.dynamic_slice_in_dim(skip_gain, side * half, half, 0)
    piece = lax.all_to_all(value_seq, "dir", split_axis=2, concat_axis=1, tiled=True)
    count = piece.shape[0]
    flat = piece.reshape(count * 2, length, half)
    result = apply_table(table_low, skip_part, flat)
    ssm_half = result.reshape(count, 2 * length, half)
    value_swapped = piece
    ssm_seq = lax.all_to_all(ssm_half, "dir", split_axis=1, concat_axis=2, tiled=True)
    ssm_out = ssm_seq.reshape(rows, chans)
    gate_pre = jnp.dot(up_act, gate_weight, preferred_element_type=jnp.float32) + gate_bias
    gated = (gate_pre * ssm_out.astype(jnp.float32)).astype(jnp.bfloat16)
    mixed = (
        inputs + jnp.dot(gated, out_weight, preferred_element_type=jnp.float32) + out_bias
    ).astype(jnp.bfloat16)
    grad_out_bias = jnp.sum(cotangent.astype(jnp.float32), axis=0)
    d_gated = jnp.einsum("td,cd->tc", cotangent, out_weight, preferred_element_type=jnp.float32)
    d_gate = (d_gated * ssm_out.astype(jnp.float32)).astype(jnp.bfloat16)
    d_ssm = (d_gated * gate_pre).astype(jnp.bfloat16)
    grad_gate_bias = jnp.sum(d_gate.astype(jnp.float32), axis=0)
    d_up = jnp.einsum("tc,hc->th", d_gate, gate_weight, preferred_element_type=jnp.float32)
    d_up_pre = (d_up * gelu_slope(up_pre)).astype(jnp.bfloat16)
    d_ssm_seq = d_ssm.reshape(seqs, length, chans)
    piece = lax.all_to_all(d_ssm_seq, "dir", split_axis=2, concat_axis=1, tiled=True)
    count = piece.shape[0]
    flat = piece.reshape(count * 2, length, half)
    result = apply_transpose(table_low, skip_part, flat)
    d_value_half = result.reshape(count, 2 * length, half)
    d_value_seq = lax.all_to_all(d_value_half, "dir", split_axis=1, concat_axis=2, tiled=True)
    flat_grad = piece.reshape(seqs * 2, length, half)
    flat_value = value_swapped.reshape(seqs * 2, length, half)
    d_table = jnp.einsum("ntc,nsc->cts", flat_grad, flat_value, preferred_element_type=jnp.float32)
    skip_half = jnp.einsum("ntc,ntc->c", flat_grad, flat_value, preferred_element_type=jnp.float32)
    grad_skip_gain = lax.dynamic_update_slice_in_dim(
        jnp.zeros((chans,), jnp.float32), skip_half, side * half, 0
    )
    grad_step_log, grad_decay_log, grad_frequency, grad_coef_real, grad_coef_imag = table_back(
        d_table
    )[0]
    d_value = d_value_seq.reshape(rows, chans)
    d_value_pre = (d_value.astype(jnp.float32) * gelu_slope(value_pre)).astype(jnp.bfloat16)
    grad_up_bias = jnp.sum(d_up_pre.astype(jnp.float32), axis=0)
    grad_value_bias = jnp.sum(d_value_pre.astype(jnp.float32), axis=0)
    normalized_gradient = jnp.einsum(
        "th,dh->td", d_up_pre, up_weight, preferred_element_type=jnp.float32
    )
    normalized_gradient = normalized_gradient + jnp.einsum(
        "tc,dc->td", d_value_pre, value_weight, preferred_element_type=jnp.float32
    )
    gain_gradient_partial = jnp.sum(normalized_gradient * standardized_input, axis=0)
    grad_bias_local = jnp.sum(normalized_gradient, axis=0)
    scaled_input = normalized_gradient * layernorm_gain
    inner = (
        scaled_input
        - jnp.mean(scaled_input, axis=1, keepdims=True)
        - standardized_input * jnp.mean(scaled_input * standardized_input, axis=1, keepdims=True)
    )
    grad_tokens = (cotangent.astype(jnp.float32) + inverse_deviation * inner).astype(jnp.bfloat16)
    grad_norm_gain, grad_norm_bias, grad_out_bias = lax.psum(
        (gain_gradient_partial, grad_bias_local, grad_out_bias), ("dp", "dir")
    )
    both_grads = jnp.concatenate([d_up_pre, d_value_pre], axis=1)
    input_full = jnp.einsum(
        "td,tk->dk", normalized_input, both_grads, preferred_element_type=jnp.float32
    )
    gate_full = jnp.einsum("th,tc->hc", up_act, d_gate, preferred_element_type=jnp.float32)
    output_full = jnp.einsum("tc,td->cd", gated, cotangent, preferred_element_type=jnp.float32)
    shares = (
        lax.psum_scatter(input_full, ("dp", "dir"), scatter_dimension=0, tiled=True),
        lax.psum_scatter(gate_full, ("dp", "dir"), scatter_dimension=0, tiled=True),
        lax.psum_scatter(output_full, ("dp", "dir"), scatter_dimension=0, tiled=True),
        lax.psum_scatter(grad_up_bias, ("dp", "dir"), scatter_dimension=0, tiled=True),
        lax.psum_scatter(grad_value_bias, ("dp", "dir"), scatter_dimension=0, tiled=True),
        lax.psum_scatter(grad_step_log, ("dp", "dir"), scatter_dimension=0, tiled=True),
        lax.psum_scatter(grad_decay_log, ("dp", "dir"), scatter_dimension=0, tiled=True),
        lax.psum_scatter(grad_frequency, ("dp", "dir"), scatter_dimension=0, tiled=True),
        lax.psum_scatter(grad_coef_real, ("dp", "dir"), scatter_dimension=0, tiled=True),
        lax.psum_scatter(grad_coef_imag, ("dp", "dir"), scatter_dimension=0, tiled=True),
        lax.psum_scatter(grad_skip_gain, ("dp", "dir"), scatter_dimension=0, tiled=True),
        lax.psum_scatter(grad_gate_bias, ("dp", "dir"), scatter_dimension=0, tiled=True),
    )
    input_share = shares[0]
    grad_up_weight = input_share[:, :hidden_width]
    grad_value_weight = input_share[:, hidden_width:]
    return (
        mixed,
        grad_tokens,
        grad_norm_gain,
        grad_norm_bias,
        grad_up_weight,
        shares[3],
        grad_value_weight,
        shares[4],
        shares[5],
        shares[6],
        shares[7],
        shares[8],
        shares[9],
        shares[10],
        shares[1],
        shares[11],
        shares[2],
        grad_out_bias,
    )


def solution(mesh):
    in_specs = (
        P(("dp", "dir"), None),
        P(),
        P(),
        P(),
        P(),
        P(),
        P(),
        P(),
        P(),
        P(),
        P(),
        P(),
        P(),
        P(),
        P(),
        P(),
        P(),
        P(("dp", "dir"), None),
    )
    out_specs = (
        P(("dp", "dir"), None),
        P(("dp", "dir"), None),
        P(),
        P(),
        P(("dp", "dir"), None),
        P(("dp", "dir")),
        P(("dp", "dir"), None),
        P(("dp", "dir")),
        P(("dp", "dir")),
        P(("dp", "dir"), None),
        P(("dp", "dir"), None),
        P(("dp", "dir"), None),
        P(("dp", "dir"), None),
        P(("dp", "dir")),
        P(("dp", "dir"), None),
        P(("dp", "dir")),
        P(("dp", "dir"), None),
        P(),
    )
    return jax.shard_map(local, mesh=mesh, in_specs=in_specs, out_specs=out_specs, check_vma=False)
```

profile of v0, /device:TPU:0, one launch (start us, length us, event | category | flops | bytes accessed | tf_op | source)
XLA Modules:
  0.0 1621.7 jit_solution(8873453828057218307)
XLA Ops:
  9.8 11.1 fusion.27
  20.9 2.6 convolution_add_fusion.2
  23.6 2.0 multiply_convert_fusion
  27.4 4.3 all-to-all-start.2
  33.7 5.7 fusion.44
  43.7 1.8 copy.93
  48.7 4.3 all-to-all-start
  53.1 1.8 copy.95
  60.0 3.0 reshape.222
  62.9 2.5 all-to-all-done
  68.8 3.3 reshape.219
  72.1 20.3 %fusion.95 = f32[768,128,128]{2,1,0:T(8,128)} fusion(bf16[4,128,768]{1,0,2:T(4,128)(2,1)S(1)} %reshape.222, bf16[4,128,768]{1,0,2:T(4,128)(2,1)} %reshape.219), kind=kOutput, calls=%fused_computation.171 | convolution fusion | flops 100663296 | bytes 51904512 | tf_op jit(solution)/shard_map/ntc,nsc->cts/dot_general | solution.py:128
  92.5 48.8 %copy.110 = f32[768,128,128]{1,2,0:T(8,128)} copy(f32[768,128,128]{2,1,0:T(8,128)} %fusion.95) | data formatting | bytes 100663296 | tf_op jit(solution)/shard_map/ntc,nsc->cts/dot_general | solution.py:128
  141.3 33.3 %fusion.1 = f32[128,128,768]{0,1,2:T(8,128)} fusion(f32[768,128,128]{2,1,0:T(8,128)} %fusion.95, f32[768,128,128]{1,2,0:T(8,128)} %copy.110, pred[]{:T(512)S(6)} %eq.3, pred[128,128]{0,1:T(8,128)(4,1)S(1)} %copy-done.32), kind=kLoop, calls=%fused_computation.4 | loop fusion | flops 50331648 | bytes 151011328 | tf_op jit(solution)/shard_map/transpose(jvp(jit(_where)))/select_n | solution.py:34
  174.5 49.3 %copy.113 = f32[128,128,768]{2,1,0:T(8,128)} copy(f32[128,128,768]{0,1,2:T(8,128)} %fusion.1) | data formatting | bytes 100663296 | tf_op jit(solution)/shard_map/transpose(jvp(jit(_where)))/select_n | solution.py:34
  223.9 109.3 %scatter_custom_fusion = f32[768,128]{0,1:T(8,128)S(1)} fusion(s32[16384]{0:T(1024)} %fusion.78, f32[16384,768]{1,0:T(8,128)} %bitcast.86, f32[]{:T(128)} %constant.42.clone.1), kind=kCustom, calls=%fused_computation.134 | custom fusion | flops 12582912 | bytes 393728 | tf_op jit(solution)/shard_map/transpose(jvp(jit(_take)))/scatter-add | solution.py:33
  334.1 133.4 %fusion.14 = (f32[768,64]{1,0:T(8,128)}, f32[768,64]{1,0:T(8,128)}, f32[768,128]{1,0:T(8,128)}, f32[768,64]{1,0:T(8,128)}, f32[768,64]{1,0:T(8,128)}) fusion(f32[768,128]{1,0:T(8,128)} %copy.115, f32[768,64]{1,0:T(8,128)} %get-tuple-element.54, f32[128]{0:T(128)S(1)} %iota_convert_fusion, f32[768,64]{1,0:T(8,128)} %get-tuple-element.53, f32[768,64]{1,0:T(8,128)} %copy.97, ...), kind=kLoop, calls=%fused_computation.21 | loop fusion | flops 156991488 | bytes 2359808 | tf_op jit(solution)/shard_map/transpose(jvp())/reduce_sum | solution.py:24
  468.7 67.9 %gather_fusion = bf16[16384,768]{1,0:T(8,128)(2,1)} fusion(bf16[768,128]{0,1:T(8,128)(2,1)S(1)} %broadcast_multiply_fusion.2, s32[16384]{0:T(1024)S(1)} %copy-done.25), kind=kCustom, calls=%fused_computation | custom fusion | bytes 50397184 | tf_op jit(solution)/shard_map/jvp(jit(_take))/gather | solution.py:33
  536.7 34.8 %copy.100 = bf16[128,128,768]{0,1,2:T(8,128)(2,1)} copy(bf16[128,128,768]{2,1,0:T(8,128)(2,1)} %bitcast.84) | data formatting | bytes 50331648 | tf_op jit(solution)/shard_map/jvp(jit(_take))/gather | solution.py:33
  571.5 32.1 %copy.99 = bf16[128,128,768]{1,0,2:T(8,128)(2,1)} copy(bf16[128,128,768]{2,1,0:T(8,128)(2,1)} %bitcast.85) | data formatting | bytes 50331648 | tf_op jit(solution)/shard_map/jvp(jit(_take))/gather | solution.py:33
  603.7 30.7 %fusion.2 = bf16[768,128,128]{1,2,0:T(8,128)(2,1)} fusion(bf16[128,128,768]{1,0,2:T(8,128)(2,1)} %copy.99, bf16[128,128,768]{0,1,2:T(8,128)(2,1)} %copy.100, pred[128,128]{0,1:T(8,128)(4,1)S(1)} %copy-done.33, pred[128,128]{0,1:T(8,128)(4,1)S(1)} %copy-done.36, pred[128,128]{0,1:T(8,128)(4,1)S(1)} %copy-done.35, pred[128,128]{0,1:T(8,128)(4,1)S(1)} %copy-done.34, ...), kind=kLoop, calls=%fused_computation.6 | loop fusion | flops 62914560 | bytes 75563008 | tf_op jit(solution)/shard_map/convert_element_type | solution.py:97
  634.4 17.4 %fusion.51 = bf16[4,128,768]{1,0,2:T(4,128)(2,1)} fusion(bf16[4,128,768]{1,0,2:T(4,128)(2,1)S(1)} %copy-done.2, bf16[768,128,128]{1,2,0:T(8,128)(2,1)} %fusion.2, f32[768]{0:T(1024)S(1)} %copy-done.42), kind=kOutput, calls=%fused_computation.80 | convolution fusion | flops 102236160 | bytes 26741760 | tf_op jit(solution)/shard_map/cts,ntc->nsc/dot_general | solution.py:44
  651.9 3.2 reshape.223
  655.1 3.7 copy.107
  658.8 4.3 all-to-all-start.3
  663.1 15.8 fusion.52
  678.9 3.0 reshape.220
  681.9 3.7 copy.102
  685.6 4.3 all-to-all-start.1
  693.8 6.7 all-to-all-done.1
  705.1 2.0 convert_reduce_fusion.1
  707.5 6.5 convert_reduce_fusion
  715.2 7.1 fusion.38
  723.4 2.7 multiply_dynamic-update-slice_fusion.1
  727.1 2.7 multiply_dynamic-update-slice_fusion
  735.5 4.4 fusion.97
  740.0 12.1 fusion.96
  752.1 2.8 fusion.50
  758.8 4.7 fusion.94
  766.3 44.8 %all-reduce.5 = (f32[768]{0:T(1024)}, f32[768]{0:T(1024)}, f32[3072]{0:T(1024)}, f32[1536]{0:T(1024)}, f32[1536]{0:T(1024)}, /*index=5*/f32[1536]{0:T(1024)}, f32[1536]{0:T(1024)S(1)}, f32[768]{0:T(1024)}) all-reduce(f32[768]{0:T(1024)} %get-tuple-element.21, ...), channel_id=1, replica_groups=mesh['dp'=16,'dir'=2] {'dp','dir'}, use_global_device_ids=true, to_apply=%region_6.7 | all-reduce | flops 11520 | bytes 92160 | tf_op jit(solution)/shard_map/psum | solution.py:155
  816.8 3.3 fusion.61
  820.0 67.8 %reduce-scatter.8.cloned.1.call-done = f32[24,4608]{1,0:T(8,128)} async-done(((f32[768,4608]{1,0:T(8,128)}), f32[24,4608]{1,0:T(8,128)}) %reduce-scatter.8.cloned.1.call-update) | async-done | bytes 442384 | tf_op jit(solution)/shard_map/reduce_scatter | solution.py:165
  891.1 96.7 %reduce-scatter.10.cloned.1.call-done = f32[48,64]{1,0:T(8,128)} async-done(((f32[1536,64]{1,0:T(8,128)}), f32[48,64]{1,0:T(8,128)}) %reduce-scatter.10.cloned.1.call-update) | async-done | bytes 12304 | tf_op jit(solution)/shard_map/reduce_scatter | solution.py:171
  987.8 100.3 %reduce-scatter.12.cloned.1.call-done = f32[48,64]{1,0:T(8,128)} async-done(((f32[1536,64]{1,0:T(8,128)}), f32[48,64]{1,0:T(8,128)}) %reduce-scatter.12.cloned.1.call-update) | async-done | bytes 12304 | tf_op jit(solution)/shard_map/reduce_scatter | solution.py:172
  1088.1 100.1 %reduce-scatter.14.cloned.1.call-done = f32[48,64]{1,0:T(8,128)} async-done(((f32[1536,64]{1,0:T(8,128)}), f32[48,64]{1,0:T(8,128)}) %reduce-scatter.14.cloned.1.call-update) | async-done | bytes 12304 | tf_op jit(solution)/shard_map/reduce_scatter | solution.py:173
  1188.2 100.2 %reduce-scatter.16.cloned.1.call-done = f32[48,64]{1,0:T(8,128)} async-done(((f32[1536,64]{1,0:T(8,128)}), f32[48,64]{1,0:T(8,128)}) %reduce-scatter.16.cloned.1.call-update) | async-done | bytes 12304 | tf_op jit(solution)/shard_map/reduce_scatter | solution.py:174
  1288.4 112.0 %reduce-scatter.20.cloned.1.call-done = f32[48,768]{1,0:T(8,128)} async-done(((f32[1536,768]{1,0:T(8,128)}), f32[48,768]{1,0:T(8,128)}) %reduce-scatter.20.cloned.1.call-update) | async-done | bytes 147472 | tf_op jit(solution)/shard_map/reduce_scatter | solution.py:167
  1400.4 214.0 %reduce-scatter.18.cloned.1.call-done = f32[96,1536]{1,0:T(8,128)} async-done(((f32[3072,1536]{1,0:T(8,128)}), f32[96,1536]{1,0:T(8,128)}) %reduce-scatter.18.cloned.1.call-update) | async-done | bytes 589840 | tf_op jit(solution)/shard_map/reduce_scatter | solution.py:166
  (167 shorter events, 57.7 us)
Async XLA Ops:
  7.2 26.5 %copy-start = (bf16[768,1536]{1,0:T(8,128)(2,1)S(1)}, bf16[768,1536]{1,0:T(8,128)(2,1)}, u32[]{:S(2)}) copy-start(bf16[768,1536]{1,0:T(8,128)(2,1)} %param.23) | copy-start | bytes 7077892
  8.5 25.2 %copy-start.37 = (f32[256]{0:T(256)}, f32[256]{0:T(256)S(1)}, u32[]{:S(2)}) copy-start(f32[256]{0:T(256)S(1)} %broadcast_multiply_fusion.5) | copy-start | bytes 3076
  9.8 23.9 %copy-start.40 = (f32[256]{0:T(256)}, f32[256]{0:T(256)S(1)}, u32[]{:S(2)}) copy-start(f32[256]{0:T(256)S(1)} %add_rsqrt_fusion) | copy-start | bytes 3076
  9.8 11.1 copy-start.44
  9.8 11.1 copy-start.45
  20.9 2.7 copy-start.19
  20.9 2.7 copy-start.10
  25.6 8.1 copy-start.7
  25.6 8.1 copy-start.26
  25.6 8.1 copy-start.28
  27.4 21.3 %all-to-all-start.2 = ((bf16[2,128,1536]{1,0,2:T(2,128)(2,1)}), bf16[2,128,1536]{1,0,2:T(2,128)(2,1)}, u32[]{:S(2)}, u32[]{:S(2)}) async-start(bf16[2,128,1536]{1,0,2:T(2,128)(2,1)} %copy.105), calls=%async_computation.2 | async-start | bytes 1572864 | tf_op jit(solution)/shard_map/all_to_all | solution.py:120
  43.7 425.0 %copy-start.30 = (f32[768]{0:T(1024)}, f32[768]{0:T(1024)S(1)}, u32[]{:S(2)}) copy-start(f32[768]{0:T(1024)S(1)} %dynamic-slice_exponential_fusion) | copy-start | bytes 9220
  45.5 9.4 copy-start.23
  45.5 10.3 copy-start.43
  45.7 12.5 copy-start.15
  46.9 11.3 copy-start.14
  48.7 16.7 %all-to-all-start = ((bf16[2,128,1536]{1,0,2:T(2,128)(2,1)}), bf16[2,128,1536]{1,0,2:T(2,128)(2,1)}, u32[]{:S(2)}, u32[]{:S(2)}) async-start(bf16[2,128,1536]{1,0,2:T(2,128)(2,1)} %copy.93), calls=%async_computation | async-start | bytes 1572864 | tf_op jit(solution)/shard_map/all_to_all | solution.py:99
  62.9 29.6 %copy-start.1 = (bf16[4,128,768]{1,0,2:T(4,128)(2,1)}, bf16[4,128,768]{1,0,2:T(4,128)(2,1)S(1)}, u32[]{:S(2)}) copy-start(bf16[4,128,768]{1,0,2:T(4,128)(2,1)S(1)} %reshape.222) | copy-start | bytes 2359300
  92.5 48.8 %copy-start.32 = (pred[128,128]{0,1:T(8,128)(4,1)S(1)}, pred[128,128]{0,1:T(8,128)(4,1)}, u32[]{:S(2)}) copy-start(pred[128,128]{0,1:T(8,128)(4,1)} %get-tuple-element.68) | copy-start | bytes 49156
  174.5 159.6 %copy-start.24 = (f32[768,64]{1,0:T(8,128)S(1)}, f32[768,64]{1,0:T(8,128)}, u32[]{:S(2)}) copy-start(f32[768,64]{1,0:T(8,128)} %copy.95) | copy-start | bytes 589828
  333.1 134.4 %copy-start.12 = (f32[768,128]{0,1:T(8,128)}, f32[768,128]{0,1:T(8,128)S(1)}, u32[]{:S(2)}) copy-start(f32[768,128]{0,1:T(8,128)S(1)} %scatter_custom_fusion) | copy-start | bytes 1179652
  334.1 134.6 %copy-start.25 = (s32[16384]{0:T(1024)S(1)}, s32[16384]{0:T(1024)}, u32[]{:S(2)}) copy-start(s32[16384]{0:T(1024)} %broadcast_clamp_fusion) | copy-start | bytes 196612
  468.7 68.0 %copy-start.13 = (f32[768,128]{0,1:T(8,128)}, f32[768,128]{0,1:T(8,128)S(1)}, u32[]{:S(2)}) copy-start(f32[768,128]{0,1:T(8,128)S(1)} %copy.98) | copy-start | bytes 1179652
  571.5 32.2 %copy-start.33 = (pred[128,128]{0,1:T(8,128)(4,1)S(1)}, pred[128,128]{0,1:T(8,128)(4,1)}, u32[]{:S(2)}) copy-start(pred[128,128]{0,1:T(8,128)(4,1)} %get-tuple-element.68) | copy-start | bytes 49156
  571.5 32.2 %copy-start.34 = (pred[128,128]{0,1:T(8,128)(4,1)S(1)}, pred[128,128]{0,1:T(8,128)(4,1)}, u32[]{:S(2)}) copy-start(pred[128,128]{0,1:T(8,128)(4,1)} %get-tuple-element.69) | copy-start | bytes 49156
  571.5 32.2 %copy-start.35 = (pred[128,128]{0,1:T(8,128)(4,1)S(1)}, pred[128,128]{0,1:T(8,128)(4,1)}, u32[]{:S(2)}) copy-start(pred[128,128]{0,1:T(8,128)(4,1)} %get-tuple-element.70) | copy-start | bytes 49156
  571.5 32.2 %copy-start.36 = (pred[128,128]{0,1:T(8,128)(4,1)S(1)}, pred[128,128]{0,1:T(8,128)(4,1)}, u32[]{:S(2)}) copy-start(pred[128,128]{0,1:T(8,128)(4,1)} %get-tuple-element.71) | copy-start | bytes 49156
  603.7 30.8 %copy-start.2 = (bf16[4,128,768]{1,0,2:T(4,128)(2,1)S(1)}, bf16[4,128,768]{1,0,2:T(4,128)(2,1)}, u32[]{:S(2)}) copy-start(bf16[4,128,768]{1,0,2:T(4,128)(2,1)} %copy-done.1) | copy-start | bytes 2359300
  603.7 30.8 %copy-start.42 = (f32[768]{0:T(1024)S(1)}, f32[768]{0:T(1024)}, u32[]{:S(2)}) copy-start(f32[768]{0:T(1024)} %dynamic_slice.23) | copy-start | bytes 9220
  658.8 26.8 %all-to-all-start.3 = ((bf16[2,256,768]{2,0,1:T(2,128)(2,1)}), bf16[2,256,768]{2,0,1:T(2,128)(2,1)}, u32[]{:S(2)}, u32[]{:S(2)}) async-start(bf16[2,256,768]{2,0,1:T(2,128)(2,1)} %copy.107), calls=%async_computation.3 | async-start | bytes 1572864 | tf_op jit(solution)/shard_map/all_to_all | solution.py:125
  685.6 14.9 all-to-all-start.1
  689.9 197.9 %reduce-scatter.8.cloned.1.call-start = ((), (), s32[]{:S(2)}) async-start(), calls=%async_computation.11 | async-start | bytes 14598144 | tf_op jit(solution)/shard_map/reduce_scatter | solution.py:165
  705.0 9.1 copy-start.17
  707.2 6.9 copy-start.16
  707.5 7.7 copy-start.8
  707.5 7.7 copy-start.27
  707.5 7.7 copy-start.29
  707.5 7.7 copy-start.38
  707.5 7.7 copy-start.41
  722.4 265.4 %reduce-scatter.10.cloned.1.call-start = ((), (), s32[]{:S(2)}) async-start(), calls=%async_computation.12 | async-start | bytes 811008 | tf_op jit(solution)/shard_map/reduce_scatter | solution.py:171
  726.1 362.0 %reduce-scatter.12.cloned.1.call-start = ((), (), s32[]{:S(2)}) async-start(), calls=%async_computation.13 | async-start | bytes 811008 | tf_op jit(solution)/shard_map/reduce_scatter | solution.py:172
  729.8 458.4 %reduce-scatter.14.cloned.1.call-start = ((), (), s32[]{:S(2)}) async-start(), calls=%async_computation.14 | async-start | bytes 811008 | tf_op jit(solution)/shard_map/reduce_scatter | solution.py:173
  732.7 555.7 %reduce-scatter.16.cloned.1.call-start = ((), (), s32[]{:S(2)}) async-start(), calls=%async_computation.15 | async-start | bytes 811008 | tf_op jit(solution)/shard_map/reduce_scatter | solution.py:174
  735.5 664.9 %reduce-scatter.20.cloned.1.call-start = ((), (), s32[]{:S(2)}) async-start(), calls=%async_computation.17 | async-start | bytes 4866048 | tf_op jit(solution)/shard_map/reduce_scatter | solution.py:167
  739.9 874.5 %reduce-scatter.18.cloned.1.call-start = ((), (), s32[]{:S(2)}) async-start(), calls=%async_computation.16 | async-start | bytes 19464192 | tf_op jit(solution)/shard_map/reduce_scatter | solution.py:166
  755.5 3.4 copy-start.39
  758.8 4.7 copy-start.18
  763.6 53.2 %copy-start.9 = (bf16[256,1536]{1,0:T(8,128)(2,1)S(1)}, bf16[256,1536]{1,0:T(8,128)(2,1)}, u32[]{:S(2)}) copy-start(bf16[256,1536]{1,0:T(8,128)(2,1)} %get-tuple-element.42) | copy-start | bytes 2359300
  (10 other events, 18.0 us)
Sparse Core Ops, SparseCore 0:
  722.5 165.2 reduce-scatter.7
  893.5 94.2 reduce-scatter.9
  993.5 94.5 reduce-scatter.11
  1093.6 94.5 reduce-scatter.13
  1193.8 94.5 reduce-scatter.15
  1294.3 106.0 reduce-scatter.19
  1408.5 205.8 reduce-scatter.17
where the time goes:
time: 1630 us; the launch traced here: 1620 us
  waiting for transfers between devices  800 us (49%)
  other arithmetic  332 us (20%)
  local copies, waits for them, and re-layouts  297 us (18%)
  matrix products  115 us (7%)
  blocking collectives  44.8 us (3%)
  starting transfers between devices  17.5 us (1%)
    reduce_scatter x1, waiting for transfers between devices, local(): lax.psum_scatter(gate_full, ('dp', 'dir'), scatter_dimension=0, tiled=True)  214 us
    gather x3, local copies, waits for them, and re-layouts, toeplitz(): table = jnp.take(kern, jnp.clip(gap, 0, length - 1), axis=1)  135 us
    reduce_sum x1, other arithmetic, kernel_rows(): coef_imag[:, :, None] * jnp.sin(phase)  133 us
    reduce_scatter x1, waiting for transfers between devices, local(): lax.psum_scatter(output_full, ('dp', 'dir'), scatter_dimension=0, tiled=T...  112 us
    scatter-add x1, other arithmetic, toeplitz(): table = jnp.take(kern, jnp.clip(gap, 0, length - 1), axis=1)  109 us
    reduce_scatter x1, waiting for transfers between devices, local(): lax.psum_scatter(grad_frequency, ('dp', 'dir'), scatter_dimension=0, tile...  100 us
    reduce_scatter x1, waiting for transfers between devices, local(): lax.psum_scatter(grad_coef_imag, ('dp', 'dir'), scatter_dimension=0, tile...  100 us
    reduce_scatter x1, waiting for transfers between devices, local(): lax.psum_scatter(grad_coef_real, ('dp', 'dir'), scatter_dimension=0, tile...  100 us
  transfers between devices with their start and end apart: 11, of which 9 were waited for; matrix products, arithmetic and copies ran while one was open for 7% of the time, Pallas kernels for 0%

commit v1 on v0

v1 whole, which is shorter than its diff:
```python
import math

import jax
import jax.numpy as jnp
import numpy as np
from jax import lax
from jax.sharding import PartitionSpec as P

SEQ_LEN = 128
AXES = ("dp", "dir")

eps = 1e-05
root_half = 0.7071067811865476
inv_root_two_pi = 0.3989422804014327
bf16 = jnp.bfloat16
f32 = jnp.float32


def gelu_slope(v):
    return 0.5 * (1.0 + lax.erf(v * root_half)) + v * inv_root_two_pi * jnp.exp(-0.5 * v * v)


def kernel_rows(step_log, decay_log, frequency, coef_real, coef_imag, length):
    delta = jnp.exp(step_log)[:, None, None]
    lags = jnp.arange(length).astype(f32)[None, None, :]
    rate = jnp.exp(decay_log)[:, :, None]
    phase = frequency[:, :, None] * delta * lags
    damp = jnp.exp(-rate * delta * lags)
    terms = damp * (coef_real[:, :, None] * jnp.cos(phase) - coef_imag[:, :, None] * jnp.sin(phase))
    return delta[:, :, 0] * jnp.sum(terms, axis=1)


def fourier(length):
    freq = np.arange(length)[:, None] + 0.5
    time = np.arange(length)[None, :]
    angle = np.pi * freq * time / length
    ahead = np.concatenate([np.cos(angle), -np.sin(angle)], axis=0)
    back = np.concatenate([np.cos(angle), -np.sin(angle)], axis=0).T / length
    return ahead.astype(np.float32), back.astype(np.float32)


def local(
    n_dp,
    n_dir,
    tokens,
    layernorm_gain,
    layernorm_bias,
    up_weight,
    up_bias,
    value_weight,
    value_bias,
    step_log,
    decay_log,
    frequency,
    coef_real,
    coef_imag,
    skip_gain,
    gate_weight,
    gate_bias,
    out_weight,
    out_bias,
    cotangent,
):
    rows, width = tokens.shape
    chans = value_weight.shape[1]
    hidden = up_weight.shape[1]
    length = SEQ_LEN
    seqs = rows // length
    n = n_dp * n_dir
    nbits = int(math.log2(n))
    me = lax.axis_index("dp") * n_dir + lax.axis_index("dir")
    bit = [(me >> b) & 1 for b in range(nbits)]
    X, C, Y = 0, 1, 2
    rest = list(range(3, nbits))
    highest = lax.Precision.HIGH

    def swap(a, b):
        return lax.ppermute(a, AXES, [(j, j ^ (1 << b)) for j in range(n)])

    def part(a, which):
        half = a.shape[0] // 2
        return lax.dynamic_slice_in_dim(a, which * half, half, 0)

    def ordered(a, order):
        a = a.reshape((2,) * nbits + (a.shape[0] // n,) + a.shape[1:])
        axes = [nbits - 1 - b for b in order] + list(range(nbits, a.ndim))
        a = a.transpose(axes)
        return a.reshape((-1,) + a.shape[nbits + 1 :])

    def reduce_rest(keep, recv, order):
        for b in order:
            send = part(keep, 1 - bit[b]) + part(recv, 1 - bit[b])
            keep, recv = part(keep, bit[b]) + part(recv, bit[b]), swap(send, b)
        return keep.astype(f32) + recv.astype(f32)

    def grad_scatter(lhs, rhs, order):
        lhs_in = swap(part(lhs, 1 - bit[C]), C)
        lhs_own = part(lhs, bit[C])
        rhs_in = swap(rhs, C)
        lhs2 = jnp.concatenate([lhs_own, lhs_in], axis=1)
        rhs2 = jnp.concatenate([rhs, rhs_in], axis=0)
        b = order[1]
        send = jnp.dot(part(lhs2, 1 - bit[b]), rhs2, preferred_element_type=f32).astype(bf16)
        recv = swap(send, b)
        keep = jnp.dot(part(lhs2, bit[b]), rhs2, preferred_element_type=f32).astype(bf16)
        return reduce_rest(keep, recv, order[2:])

    own = chans // n
    mine = [
        lax.dynamic_slice_in_dim(p, me * own, own, 0)
        for p in (step_log, decay_log, frequency, coef_real, coef_imag)
    ]
    kern_own, kern_back = jax.vjp(lambda p: kernel_rows(*p, length), tuple(mine))
    kern = kern_own.astype(bf16).reshape((1,) * nbits + (own, length))
    for b in rest[::-1] + [Y, X, C]:
        other = swap(kern, b)
        axis = nbits - 1 - b
        kern = jnp.where(
            bit[b] == 1,
            jnp.concatenate([other, kern], axis=axis),
            jnp.concatenate([kern, other], axis=axis),
        )
    kern = kern.reshape(chans, length)

    ahead, back = fourier(length)
    ahead_all = jnp.asarray(np.kron(np.eye(seqs), ahead).astype(np.float32))
    back_all = jnp.asarray(np.kron(np.eye(seqs), back).astype(np.float32))
    ahead, back = jnp.asarray(ahead), jnp.asarray(back)
    turn = jnp.where(jnp.arange(chans) < chans // 2, 1.0, -1.0).astype(f32)

    def spectrum(a):
        s = jnp.dot(ahead_all, a.astype(f32), precision=highest).reshape(seqs, 2, length, chans)
        return s[:, 0], s[:, 1]

    def unspectrum(re, im):
        s = jnp.stack([re, im], axis=1).reshape(seqs * 2 * length, chans)
        return jnp.dot(back_all, s, precision=highest)

    kern_hat = lax.dot_general(
        ahead, kern.astype(f32), (((1,), (1,)), ((), ())), precision=highest
    ).reshape(2, length, chans)
    kr, ki = kern_hat[0], kern_hat[1] * turn

    inputs = tokens.astype(f32)
    average = jnp.mean(inputs, axis=1, keepdims=True)
    centered = inputs - average
    deviation = lax.rsqrt(jnp.mean(centered * centered, axis=1, keepdims=True) + eps)
    xhat = centered * deviation
    normed = (xhat * layernorm_gain + layernorm_bias).astype(bf16)
    up_pre = jnp.dot(normed, up_weight, preferred_element_type=f32) + up_bias
    up_act = jax.nn.gelu(up_pre, approximate=False).astype(bf16)
    value_pre = jnp.dot(normed, value_weight, preferred_element_type=f32) + value_bias
    value_act = jax.nn.gelu(value_pre, approximate=False).astype(bf16)
    gate_pre = jnp.dot(up_act, gate_weight, preferred_element_type=f32) + gate_bias
    d_gated = lax.dot_general(
        cotangent, out_weight, (((1,), (1,)), ((), ())), preferred_element_type=f32
    )
    vr, vi = spectrum(value_act)
    ssm_out = (
        unspectrum(kr * vr - ki * vi, kr * vi + ki * vr) + skip_gain * value_act.astype(f32)
    ).astype(bf16)
    ssm_wide = ssm_out.astype(f32)
    gated = (gate_pre * ssm_wide).astype(bf16)
    d_gate = (d_gated * ssm_wide).astype(bf16)
    d_ssm = (d_gated * gate_pre).astype(bf16)

    gate_order = [C, X, Y] + rest
    gate_share = grad_scatter(ordered(up_act.T, gate_order), d_gate, gate_order)
    out_order = [C] + rest + [X, Y]
    out_share = grad_scatter(ordered(gated.T, out_order), cotangent, out_order)

    dr, di = spectrum(d_ssm)
    d_value = (
        unspectrum(kr * dr + ki * di, kr * di - ki * dr) + skip_gain * d_ssm.astype(f32)
    )
    gr = jnp.sum(dr * vr + di * vi, axis=0)
    gi = jnp.sum(di * vr - dr * vi, axis=0) * turn
    grad_kern = lax.dot_general(
        jnp.concatenate([gr, gi], axis=0), back, (((0,), (1,)), ((), ())), precision=highest
    )
    kern_order = [C, X, Y] + rest
    grad_kern = ordered(grad_kern, kern_order)
    b = kern_order[0]
    grad_kern = reduce_rest(part(grad_kern, bit[b]), swap(part(grad_kern, 1 - bit[b]), b), kern_order[1:])

    d_up = lax.dot_general(
        d_gate, gate_weight, (((1,), (1,)), ((), ())), preferred_element_type=f32
    )
    d_up_pre = (d_up * gelu_slope(up_pre)).astype(bf16)
    d_value_pre = (d_value.astype(bf16).astype(f32) * gelu_slope(value_pre)).astype(bf16)
    both = jnp.concatenate([d_up_pre, d_value_pre], axis=1)
    input_order = [C, Y, X] + rest
    input_share = grad_scatter(ordered(normed.T, input_order), both, input_order)

    d_normed = lax.dot_general(
        d_up_pre, up_weight, (((1,), (1,)), ((), ())), preferred_element_type=f32
    ) + lax.dot_general(
        d_value_pre, value_weight, (((1,), (1,)), ((), ())), preferred_element_type=f32
    )
    scaled = d_normed * layernorm_gain
    inner = (
        scaled
        - jnp.mean(scaled, axis=1, keepdims=True)
        - xhat * jnp.mean(scaled * xhat, axis=1, keepdims=True)
    )
    grad_tokens = (cotangent.astype(f32) + deviation * inner).astype(bf16)
    mixed = (
        inputs + jnp.dot(gated, out_weight, preferred_element_type=f32) + out_bias
    ).astype(bf16)

    vectors = [
        jnp.sum(d_normed * xhat, axis=0),
        jnp.sum(d_normed, axis=0),
        jnp.sum(cotangent.astype(f32), axis=0),
        jnp.sum(d_up_pre.astype(f32), axis=0),
        jnp.sum(d_value_pre.astype(f32), axis=0),
        jnp.sum(d_gate.astype(f32), axis=0),
        jnp.sum(d_ssm.astype(f32) * value_act.astype(f32), axis=0),
    ]
    packed = jnp.concatenate(vectors).reshape(-1, 128)
    for b in range(nbits):
        packed = packed + swap(packed, b)
    packed = packed.reshape(-1)
    sums, at = [], 0
    for v in vectors:
        sums.append(packed[at : at + v.shape[0]])
        at += v.shape[0]

    def share(v):
        size = v.shape[0] // n
        return lax.dynamic_slice_in_dim(v, me * size, size, 0)

    steps, decays, frequencies, reals, imags = kern_back(grad_kern)[0]
    return (
        mixed,
        grad_tokens,
        sums[0],
        sums[1],
        input_share[:, :hidden],
        share(sums[3]),
        input_share[:, hidden:],
        share(sums[4]),
        steps,
        decays,
        frequencies,
        reals,
        imags,
        share(sums[6]),
        gate_share,
        share(sums[5]),
        out_share,
        sums[2],
    )


def solution(mesh):
    n_dp, n_dir = mesh.shape["dp"], mesh.shape["dir"]
    split, whole = P(AXES), P()
    in_specs = (split,) + (whole,) * 16 + (split,)
    out_specs = (split, split, whole, whole) + (split,) * 13 + (whole,)

    def run(*args):
        return local(n_dp, n_dir, *args)

    return jax.shard_map(run, mesh=mesh, in_specs=in_specs, out_specs=out_specs, check_vma=False)
```

time: 1630 us -> 291 us (0.18)
  waiting for transfers between devices: 800 us -> 103 us
  other arithmetic: 332 us -> 36.3 us
  local copies, waits for them, and re-layouts: 297 us -> 48.3 us
  matrix products: 115 us -> 60.1 us
  blocking collectives: 44.8 us -> 0 us
  starting transfers between devices: 17.5 us -> 36.4 us
    reduce_scatter x7 -> x0, waiting for transfers between devices: 791 us -> none  [the longest x1 214 us: local(): lax.psum_scatter(gate_full, ('dp', 'dir'), scatter_dimension=0, tiled=True)]
    gather x3 -> x0, local copies, waits for them, and re-layouts: 135 us -> none  [toeplitz(): table = jnp.take(kern, jnp.clip(gap, 0, length - 1), axis=1)]
    reduce_sum x1, other arithmetic: 133 us -> 9.83 us  [kernel_rows(): coef_imag[:, :, None] * jnp.sin(phase)]
    scatter-add x1 -> x0, other arithmetic: 109 us -> none  [toeplitz(): table = jnp.take(kern, jnp.clip(gap, 0, length - 1), axis=1)]
    ppermute x0 -> x33, waiting for transfers between devices: none -> 103 us  [swap(): return lax.ppermute(a, AXES, [(j, j ^ 1 << b) for j in range(n)])]
    dot_general x14 -> x21, matrix products: 115 us -> 60.1 us  [the longest x1 11.7 us: local(): up_pre = jnp.dot(normed, up_weight, preferred_element_type=f32) + up_bias]
    select_n x1, local copies, waits for them, and re-layouts: 49.3 us -> 0.03 us  [local(): jnp.where(bit[b] == 1, jnp.concatenate([other, kern], axis=axis), jnp.con...]
    dot_general x1 -> x0, local copies, waits for them, and re-layouts: 48.8 us -> none  [local(): jnp.einsum('ntc,nsc->cts', flat_grad, flat_value, preferred_element_type=...]
  transfers between devices with their start and end apart: 11 -> 33, of which waited for: 9 -> 18; matrix products, arithmetic and copies ran while one was open for 7% -> 47% of each run, Pallas kernels for 0% -> 0%
where the time goes in v1:
time: 291 us; the launch traced here: 286 us
  waiting for transfers between devices  103 us (35%)
  matrix products  60.1 us (21%)
  local copies, waits for them, and re-layouts  48.3 us (17%)
  starting transfers between devices  36.4 us (13%)
  other arithmetic  36.3 us (12%)
    ppermute x33, waiting for transfers between devices, swap(): return lax.ppermute(a, AXES, [(j, j ^ 1 << b) for j in range(n)])  103 us
    ppermute x33, starting transfers between devices, swap(): return lax.ppermute(a, AXES, [(j, j ^ 1 << b) for j in range(n)])  36.4 us
    unnamed x125, local copies, waits for them, and re-layouts  21.2 us
    dot_general x1, matrix products, local(): up_pre = jnp.dot(normed, up_weight, preferred_element_type=f32) + up_bias  11.7 us
    reduce_sum x1, other arithmetic, kernel_rows(): coef_imag[:, :, None] * jnp.sin(phase)  9.83 us
    dot_general x1, matrix products, local(): jnp.dot(up_act, gate_weight, preferred_element_type=f32) + gate_bias  8.67 us
    dot_general x3, matrix products, grad_scatter(): jnp.dot(part(lhs2, 1 - bit[b]), rhs2, preferred_element_type=f32)  7.95 us
    dot_general x3, matrix products, grad_scatter(): jnp.dot(part(lhs2, bit[b]), rhs2, preferred_element_type=f32).astype(bf16)  6.19 us
  transfers between devices with their start and end apart: 33, of which 18 were waited for; matrix products, arithmetic and copies ran while one was open for 47% of the time, Pallas kernels for 0%

profile of v1, /device:TPU:0, one launch (start us, length us, event | category | flops | bytes accessed | tf_op | source)
XLA Modules:
  0.0 285.5 jit_solution(15169086258203842036)
XLA Ops:
  3.8 11.7 %fusion.9 = (bf16[3072,256]{0,1:T(8,128)(2,1)}, f32[256,3072]{1,0:T(8,128)S(1)}) fusion(f32[3072]{0:T(1024)} %param.26, bf16[768,3072]{1,0:T(8,128)(2,1)} %param.25, bf16[256,768]{1,0:T(8,128)(2,1)} %param.22, f32[768]{0:T(1024)} %param.24, f32[768]{0:T(1024)} %param.23, f32[256]{0:T(256)S(1)} %add_rsqrt_fusion, f32[256]{0:T(256)S(1)} %broadcast_multiply_fusion.5), kind=kOutput, calls=%fused_computation.19 | convolution fusion | flops 1261043712 | bytes 9850880 | tf_op jit(solution)/shard_map/dot_general | solution.py:150
  17.3 8.7 %convolution_add_fusion.3 = f32[256,1536]{1,0:T(8,128)S(1)} fusion(bf16[3072,1536]{1,0:T(8,128)(2,1)S(1)} %copy-done.48, f32[256,3072]{1,0:T(8,128)S(1)} %get-tuple-element.102, f32[1536]{0:T(1024)S(1)} %copy-done.50), kind=kOutput, calls=%fused_computation.57 | convolution fusion | flops 2467430400 | bytes 14161920 | tf_op jit(solution)/shard_map/dot_general | solution.py:154
  26.0 5.8 %fusion.45 = (f32[1536]{0:T(1024)}, bf16[256,1536]{1,0:T(8,128)(2,1)S(1)}, bf16[256,1536]{1,0:T(8,128)(2,1)S(1)}, f32[256,1536]{1,0:T(8,128)}) fusion(f32[256,1536]{1,0:T(8,128)S(1)} %convolution_add_fusion.3, f32[256,1536]{1,0:T(8,128)S(1)} %convolution_add_fusion.2, bf16[256,768]{1,0:T(8,128)(2,1)S(1)} %copy-done.25, bf16[1536,768]{1,0:T(8,128)(2,1)S(1)} %copy-done), kind=kOutput, calls=%fused_computation.88 | convolution fusion | flops 631896576 | bytes 9050112 | tf_op jit(solution)/shard_map/dot_general | solution.py:155
  38.2 2.6 copy.95
  40.8 2.7 copy.96
  43.5 2.6 constant_dynamic-slice_fusion.1
  51.8 1.8 constant_dynamic-update-slice_fusion.2
  54.7 2.5 collective-permute-start.17
  57.4 5.3 %collective-permute-done.17 = f32[384,128]{1,0:T(8,128)S(1)} collective-permute-done((f32[384,128]{1,0:T(8,128)S(1)}, f32[384,128]{1,0:T(8,128)S(1)}, u32[]{:S(2)}, u32[]{:S(2)}) %collective-permute-start.17) | collective-permute-done | bytes 196640 | tf_op jit(solution)/shard_map/ppermute | solution.py:78
  62.7 1.8 collective-permute-start.18
  65.5 1.9 collective-permute-done.18
  67.4 1.9 collective-permute-start.19
  69.4 2.1 collective-permute-done.19
  71.6 3.1 %collective-permute-start.20 = (f32[48,128]{1,0:T(8,128)S(1)}, f32[48,128]{1,0:T(8,128)S(1)}, u32[]{:S(2)}, u32[]{:S(2)}) collective-permute-start(f32[48,128]{1,0:T(8,128)S(1)} %dynamic-slice_add_fusion.21), channel_id=1, source_target_pairs={{0,16},{1,17},{2,18},{3,19},{4,20},{5,21},{6,22},{7,23},{8,24},{9,... | collective-permute-start | bytes 73736 | tf_op jit(solution)/shard_map/ppermute | solution.py:78
  74.7 1.8 constant_dynamic-update-slice_fusion.1
  77.2 9.8 %fusion.50 = (f32[48,64]{1,0:T(8,128)}, f32[48,64]{1,0:T(8,128)}, f32[48,128]{1,0:T(8,128)S(1)}, f32[48,64]{1,0:T(8,128)S(1)}, f32[48,64]{1,0:T(8,128)S(1)}) fusion(f32[48,128]{1,0:T(8,128)S(1)} %get-tuple-element.38, f32[48,64]{1,0:T(8,128)S(1)} %get-tuple-element.94, f32[128]{0:T(128)S(1)} %iota_convert_fusion, f32[48,64]{1,0:T(8,128)S(1)} %get-tuple-element.93, ...), kind=kLoop, calls=%fused_computation.93 | loop fusion | flops 9811968 | bytes 147968 | tf_op jit(solution)/shard_map/transpose(jvp())/reduce_sum | solution.py:29
  87.2 3.0 %collective-permute-start = (bf16[1,1,1,1,1,48,128]{6,5,0,1,2,4,3:T(8,128)(2,1)S(1)}, bf16[1,1,1,1,1,48,128]{6,5,0,1,2,4,3:T(8,128)(2,1)S(1)}, u32[]{:S(2)}, u32[]{:S(2)}) collective-permute-start(bf16[1,1,1,1,1,48,128]{6,5,0,1,2,4,3:T(8,128)(2,1)S(1)} %fusion.153), channel_id=1, source_target_pairs={{0,16},{1,17},{2,18},{3,19},{4,20},{5,21},{6,22},{7,23},{8,24},{9,... | collective-permute-start | bytes 36872 | tf_op jit(solution)/shard_map/ppermute | solution.py:78
  91.9 1.6 collective-permute-start.1
  93.5 2.2 collective-permute-done.1
  95.8 1.6 collective-permute-start.2
  97.4 2.5 collective-permute-done.2
  101.5 3.1 %collective-permute-done.3 = bf16[2,2,2,1,1,48,128]{6,5,0,1,2,4,3:T(8,128)(2,1)S(1)} collective-permute-done((bf16[2,2,2,1,1,48,128]{6,5,0,1,2,4,3:T(8,128)(2,1)S(1)}, bf16[2,2,2,1,1,48,128]{6,5,0,1,2,4,3:T(8,128)(2,1)S(1)}, u32[]{:S(2)}, u32[]{:S(2)}) %collective-permute-start.3) | collective-permute-done | bytes 98336 | tf_op jit(solution)/shard_map/ppermute | solution.py:78
  113.0 3.5 %convert_reduce_fusion.1 = (f32[1536]{0:T(1024)S(1)}, bf16[256,1536]{1,0:T(8,128)(2,1)}, bf16[256,1536]{1,0:T(8,128)(2,1)}, f32[1536,256]{0,1:T(8,128)}) fusion(f32[256,1536]{1,0:T(8,128)S(1)} %copy-done.22, bf16[256,1536]{1,0:T(8,128)(2,1)S(1)} %copy-done.14, f32[1536]{0:T(1024)S(1)} %copy-done.36, f32[512,1536]{1,0:T(8,128)S(1)} %bitcast.234, ...), kind=kOutput, calls=%fused_computation.132 | convolution fusion | flops 1211496960 | bytes 9187328 | tf_op jit(solution)/shard_map/dot_general | solution.py:137
  116.6 5.2 %convert_reduce_fusion = (f32[3072]{0:T(1024)S(1)}, bf16[256,3072]{1,0:T(8,128)(2,1)S(1)}) fusion(f32[256,3072]{1,0:T(8,128)S(1)} %copy-done.52, bf16[256,1536]{1,0:T(8,128)(2,1)} %get-tuple-element.36, bf16[3072,1536]{1,0:T(8,128)(2,1)S(1)} %bitcast.250), kind=kOutput, calls=%fused_computation.39 | convolution fusion | flops 2425353216 | bytes 14954496 | tf_op jit(solution)/shard_map/dot_general | solution.py:186
  122.0 1.7 copy-done.11
  124.0 2.3 convert_reduce_fusion.2
  127.8 1.6 pad_maximum_fusion.3
  145.4 1.9 copy.92
  153.5 4.5 %convolution_convert_fusion.2 = bf16[768,1536]{1,0:T(8,128)(2,1)} fusion(bf16[256,1536]{1,0:T(8,128)(2,1)} %collective-permute-done.22, bf16[256,1536]{1,0:T(8,128)(2,1)} %get-tuple-element.36, s32[]{:T(128)S(6)} %select_n.365, bf16[1536,256]{1,0:T(8,128)(2,1)S(1)} %copy-done.27, bf16[1536,256]{1,0:T(8,128)(2,1)} %collective-permute-done.21), kind=kOutput, calls=%fused_computation.9 | convolution fusion | flops 1213857792 | bytes 5505028 | tf_op jit(solution)/shard_map/dot_general | solution.py:103
  158.5 4.6 %fusion.67 = bf16[1536,256]{0,1:T(8,128)(2,1)} fusion(f32[256,1536]{1,0:T(8,128)S(1)} %copy-done.8, f32[1536,256]{0,1:T(8,128)S(1)} %copy-done.6, f32[256,1536]{1,0:T(8,128)S(1)} %copy-done.12, f32[1536]{0:T(1024)S(1)} %copy-done.36), kind=kLoop, calls=%fused_computation.116 | loop fusion | flops 28311552 | bytes 5511168 | tf_op jit(solution)/shard_map/convert_element_type | solution.py:163
  163.1 2.4 copy.98
  169.4 2.3 collective-permute-done.8
  171.7 2.9 %collective-permute-start.9 = (f32[78,128]{1,0:T(8,128)S(1)}, f32[78,128]{1,0:T(8,128)S(1)}, u32[]{:S(2)}, u32[]{:S(2)}) collective-permute-start(f32[78,128]{1,0:T(8,128)S(1)} %add.388), channel_id=1, source_target_pairs={{0,16},{1,17},{2,18},{3,19},{4,20},{5,21},{6,22},{7,23},{8,24},{9,... | collective-permute-start | bytes 119816 | tf_op jit(solution)/shard_map/ppermute | solution.py:78
  174.6 3.0 %convolution_convert_fusion = bf16[192,4608]{1,0:T(8,128)(2,1)S(1)} fusion(bf16[256,4608]{1,0:T(8,128)(2,1)} %collective-permute-done.11, bf16[256,1536]{1,0:T(8,128)(2,1)S(1)} %get-tuple-element.100, bf16[256,3072]{1,0:T(8,128)(2,1)S(1)} %copy-done.24, s32[]{:T(128)S(6)} %select_n.343, bf16[384,256]{1,0:T(8,128)(2,1)S(1)} %copy-done.34, ...), kind=kOutput, calls=%fused_computation | convolution fusion | flops 921403392 | bytes 6881284 | tf_op jit(solution)/shard_map/dot_general | solution.py:103
  180.3 1.6 collective-permute-start.29
  184.2 2.9 %convolution_convert_fusion.3 = bf16[768,1536]{1,0:T(8,128)(2,1)S(1)} fusion(bf16[256,1536]{1,0:T(8,128)(2,1)} %collective-permute-done.22, bf16[256,1536]{1,0:T(8,128)(2,1)} %get-tuple-element.36, s32[]{:T(128)S(6)} %select_n.363, bf16[1536,256]{1,0:T(8,128)(2,1)S(1)} %copy-done.28, bf16[1536,256]{1,0:T(8,128)(2,1)} %collective-permute-done.21), kind=kOutput, calls=%fused_computation.10 | convolution fusion | flops 1213857792 | bytes 5505028 | tf_op jit(solution)/shard_map/dot_general | solution.py:105
  187.1 6.8 %collective-permute-done.29 = bf16[384,768]{1,0:T(8,128)(2,1)S(1)} collective-permute-done((bf16[384,768]{1,0:T(8,128)(2,1)S(1)}, bf16[384,768]{1,0:T(8,128)(2,1)S(1)}, u32[]{:S(2)}, u32[]{:S(2)}) %collective-permute-start.29) | collective-permute-done | bytes 589856 | tf_op jit(solution)/shard_map/ppermute | solution.py:78
  194.4 2.8 convolution_convert_fusion.1
  197.3 14.1 %collective-permute-done.23 = bf16[768,1536]{1,0:T(8,128)(2,1)} collective-permute-done((bf16[768,1536]{1,0:T(8,128)(2,1)}, bf16[768,1536]{1,0:T(8,128)(2,1)}, u32[]{:S(2)}, u32[]{:S(2)}) %collective-permute-start.23) | collective-permute-done | bytes 2359328 | tf_op jit(solution)/shard_map/ppermute | solution.py:78
  211.4 2.3 dynamic-slice_add_fusion.1
  214.2 3.8 %collective-permute-done.12 = bf16[192,4608]{1,0:T(8,128)(2,1)S(1)} collective-permute-done((bf16[192,4608]{1,0:T(8,128)(2,1)S(1)}, bf16[192,4608]{1,0:T(8,128)(2,1)S(1)}, u32[]{:S(2)}, u32[]{:S(2)}) %collective-permute-start.12) | collective-permute-done | bytes 1769504 | tf_op jit(solution)/shard_map/ppermute | solution.py:78
  218.5 2.5 collective-permute-start.13
  222.3 17.2 %collective-permute-done.31 = bf16[96,768]{1,0:T(8,128)(2,1)S(1)} collective-permute-done((bf16[96,768]{1,0:T(8,128)(2,1)S(1)}, bf16[96,768]{1,0:T(8,128)(2,1)S(1)}, u32[]{:S(2)}, u32[]{:S(2)}) %collective-permute-start.31) | collective-permute-done | bytes 147488 | tf_op jit(solution)/shard_map/ppermute | solution.py:78
  240.3 2.5 collective-permute-done.24
  246.2 16.4 %collective-permute-done.25 = bf16[192,1536]{1,0:T(8,128)(2,1)S(1)} collective-permute-done((bf16[192,1536]{1,0:T(8,128)(2,1)S(1)}, bf16[192,1536]{1,0:T(8,128)(2,1)S(1)}, u32[]{:S(2)}, u32[]{:S(2)}) %collective-permute-start.25) | collective-permute-done | bytes 589856 | tf_op jit(solution)/shard_map/ppermute | solution.py:78
  262.9 7.5 %collective-permute-done.14 = bf16[48,4608]{1,0:T(8,128)(2,1)S(1)} collective-permute-done((bf16[48,4608]{1,0:T(8,128)(2,1)S(1)}, bf16[48,4608]{1,0:T(8,128)(2,1)S(1)}, u32[]{:S(2)}, u32[]{:S(2)}) %collective-permute-start.14) | collective-permute-done | bytes 442400 | tf_op jit(solution)/shard_map/ppermute | solution.py:78
  270.6 10.2 %collective-permute-done.26 = bf16[96,1536]{1,0:T(8,128)(2,1)S(1)} collective-permute-done((bf16[96,1536]{1,0:T(8,128)(2,1)S(1)}, bf16[96,1536]{1,0:T(8,128)(2,1)S(1)}, u32[]{:S(2)}, u32[]{:S(2)}) %collective-permute-start.26) | collective-permute-done | bytes 294944 | tf_op jit(solution)/shard_map/ppermute | solution.py:78
  281.7 2.1 collective-permute-done.15
  (249 shorter events, 74.7 us)
Async XLA Ops:
  0.7 25.3 %copy-start = (bf16[1536,768]{1,0:T(8,128)(2,1)S(1)}, bf16[1536,768]{1,0:T(8,128)(2,1)}, u32[]{:S(2)}) copy-start(bf16[1536,768]{1,0:T(8,128)(2,1)} %param.37) | copy-start | bytes 7077892
  0.7 74.0 %collective-permute-start.28 = (bf16[256,768]{1,0:T(8,128)(2,1)}, bf16[256,768]{1,0:T(8,128)(2,1)}, u32[]{:S(2)}, u32[]{:S(2)}) collective-permute-start(bf16[256,768]{1,0:T(8,128)(2,1)} %param.39), channel_id=1, source_target_pairs={{0,2},{1,3},{2,0},{3,1},{4,6},{5,7},{6,4},{7,5},{8,10},{9,11},{10,... | collective-permute-start | bytes 1179656 | tf_op jit(solution)/shard_map/ppermute | solution.py:78
  3.8 11.8 %copy-start.43 = (f32[256]{0:T(256)}, f32[256]{0:T(256)S(1)}, u32[]{:S(2)}) copy-start(f32[256]{0:T(256)S(1)} %add_rsqrt_fusion) | copy-start | bytes 3076
  3.8 11.8 %copy-start.5 = (bf16[256,768]{1,0:T(8,128)(2,1)S(1)}, bf16[256,768]{1,0:T(8,128)(2,1)}, u32[]{:S(2)}) copy-start(bf16[256,768]{1,0:T(8,128)(2,1)} %param.22) | copy-start | bytes 1179652
  3.8 11.8 %copy-start.18 = (bf16[768,1536]{1,0:T(8,128)(2,1)S(1)}, bf16[768,1536]{1,0:T(8,128)(2,1)}, u32[]{:S(2)}) copy-start(bf16[768,1536]{1,0:T(8,128)(2,1)} %param.27) | copy-start | bytes 7077892
  3.8 11.8 %copy-start.39 = (f32[768]{0:T(1024)S(1)}, f32[768]{0:T(1024)}, u32[]{:S(2)}) copy-start(f32[768]{0:T(1024)} %param.23) | copy-start | bytes 9220
  3.8 11.8 %copy-start.46 = (f32[768]{0:T(1024)S(1)}, f32[768]{0:T(1024)}, u32[]{:S(2)}) copy-start(f32[768]{0:T(1024)} %param.24) | copy-start | bytes 9220
  3.8 11.8 %copy-start.49 = (f32[1536]{0:T(1024)S(1)}, f32[1536]{0:T(1024)}, u32[]{:S(2)}) copy-start(f32[1536]{0:T(1024)} %param.28) | copy-start | bytes 18436
  3.8 13.4 %copy-start.48 = (bf16[3072,1536]{1,0:T(8,128)(2,1)S(1)}, bf16[3072,1536]{1,0:T(8,128)(2,1)}, u32[]{:S(2)}) copy-start(bf16[3072,1536]{1,0:T(8,128)(2,1)} %param.35) | copy-start | bytes 28311556
  38.2 15.5 %collective-permute-start.16 = (f32[768,128]{1,0:T(8,128)}, f32[768,128]{1,0:T(8,128)}, u32[]{:S(2)}, u32[]{:S(2)}) collective-permute-start(f32[768,128]{1,0:T(8,128)} %constant_dynamic-slice_fusion.3), channel_id=1, source_target_pairs={{0,2},{1,3},{2,0},{3,1},{4,6},{5,7},{6,4},{7,5},{8,10},{9,11},{10,... | collective-permute-start | bytes 1179656 | tf_op jit(solution)/shard_map/ppermute | solution.py:78
  46.1 107.4 %collective-permute-start.21 = (bf16[1536,256]{1,0:T(8,128)(2,1)}, bf16[1536,256]{1,0:T(8,128)(2,1)}, u32[]{:S(2)}, u32[]{:S(2)}) collective-permute-start(bf16[1536,256]{1,0:T(8,128)(2,1)} %get-tuple-element.52), channel_id=1, source_target_pairs={{0,2},{1,3},{2,0},{3,1},{4,6},{5,7},{6,4},{7,5},{8,10},{9,11},{10,... | collective-permute-start | bytes 2359304 | tf_op jit(solution)/shard_map/ppermute | solution.py:78
  51.8 12.7 %copy-start.41 = (f32[48]{0:T(128)}, f32[48]{0:T(128)S(1)}, u32[]{:S(2)}) copy-start(f32[48]{0:T(128)S(1)} %dynamic-slice_exponential_fusion) | copy-start | bytes 580
  54.7 7.9 %collective-permute-start.17 = (f32[384,128]{1,0:T(8,128)S(1)}, f32[384,128]{1,0:T(8,128)S(1)}, u32[]{:S(2)}, u32[]{:S(2)}) collective-permute-start(f32[384,128]{1,0:T(8,128)S(1)} %get-tuple-element.61), channel_id=1, source_target_pairs={{0,1},{1,0},{2,3},{3,2},{4,5},{5,4},{6,7},{7,6},{8,9},{9,8},{10,11... | collective-permute-start | bytes 589832 | tf_op jit(solution)/shard_map/ppermute | solution.py:78
  62.7 4.7 %collective-permute-start.18 = (f32[192,128]{1,0:T(8,128)S(1)}, f32[192,128]{1,0:T(8,128)S(1)}, u32[]{:S(2)}, u32[]{:S(2)}) collective-permute-start(f32[192,128]{1,0:T(8,128)S(1)} %get-tuple-element.72), channel_id=1, source_target_pairs={{0,4},{1,5},{2,6},{3,7},{4,0},{5,1},{6,2},{7,3},{8,12},{9,13},{10,... | collective-permute-start | bytes 294920 | tf_op jit(solution)/shard_map/ppermute | solution.py:78
  67.4 4.2 %collective-permute-start.19 = (f32[96,128]{1,0:T(8,128)S(1)}, f32[96,128]{1,0:T(8,128)S(1)}, u32[]{:S(2)}, u32[]{:S(2)}) collective-permute-start(f32[96,128]{1,0:T(8,128)S(1)} %get-tuple-element.74), channel_id=1, source_target_pairs={{0,8},{1,9},{2,10},{3,11},{4,12},{5,13},{6,14},{7,15},{8,0},{9,1},... | collective-permute-start | bytes 147464 | tf_op jit(solution)/shard_map/ppermute | solution.py:78
  71.6 15.5 %copy-start.42 = (f32[48]{0:T(128)S(1)}, f32[48]{0:T(128)}, u32[]{:S(2)}) copy-start(f32[48]{0:T(128)} %copy-done.41) | copy-start | bytes 580
  71.6 4.9 %collective-permute-start.20 = (f32[48,128]{1,0:T(8,128)S(1)}, f32[48,128]{1,0:T(8,128)S(1)}, u32[]{:S(2)}, u32[]{:S(2)}) collective-permute-start(f32[48,128]{1,0:T(8,128)S(1)} %dynamic-slice_add_fusion.21), channel_id=1, source_target_pairs={{0,16},{1,17},{2,18},{3,19},{4,20},{5,21},{6,22},{7,23},{8,24},{9,... | collective-permute-start | bytes 73736 | tf_op jit(solution)/shard_map/ppermute | solution.py:78
  77.2 27.5 %copy-start.30 = (f32[48,64]{1,0:T(8,128)S(1)}, f32[48,64]{1,0:T(8,128)}, u32[]{:S(2)}) copy-start(f32[48,64]{1,0:T(8,128)} %copy.101) | copy-start | bytes 36868
  77.2 27.5 %copy-start.32 = (f32[48,64]{1,0:T(8,128)S(1)}, f32[48,64]{1,0:T(8,128)}, u32[]{:S(2)}) copy-start(f32[48,64]{1,0:T(8,128)} %copy.102) | copy-start | bytes 36868
  87.1 19.2 %copy-start.35 = (f32[256,128]{1,0:T(8,128)S(1)}, f32[256,128]{1,0:T(8,128)}, u32[]{:S(2)}) copy-start(f32[256,128]{1,0:T(8,128)} %constant.45.clone) | copy-start | bytes 393220
  87.2 4.7 %collective-permute-start = (bf16[1,1,1,1,1,48,128]{6,5,0,1,2,4,3:T(8,128)(2,1)S(1)}, bf16[1,1,1,1,1,48,128]{6,5,0,1,2,4,3:T(8,128)(2,1)S(1)}, u32[]{:S(2)}, u32[]{:S(2)}) collective-permute-start(bf16[1,1,1,1,1,48,128]{6,5,0,1,2,4,3:T(8,128)(2,1)S(1)} %fusion.153), channel_id=1, source_target_pairs={{0,16},{1,17},{2,18},{3,19},{4,20},{5,21},{6,22},{7,23},{8,24},{9,... | collective-permute-start | bytes 36872 | tf_op jit(solution)/shard_map/ppermute | solution.py:78
  91.9 3.8 %collective-permute-start.1 = (bf16[2,1,1,1,1,48,128]{6,5,0,1,2,4,3:T(8,128)(2,1)S(1)}, bf16[2,1,1,1,1,48,128]{6,5,0,1,2,4,3:T(8,128)(2,1)S(1)}, u32[]{:S(2)}, u32[]{:S(2)}) collective-permute-start(bf16[2,1,1,1,1,48,128]{6,5,0,1,2,4,3:T(8,128)(2,1)S(1)} %maximum_select_fusion.6), channel_id=1, source_target_pairs={{0,8},{1,9},{2,10},{3,11},{4,12},{5,13},{6,14},{7,15},{8,0},{9,1},... | collective-permute-start | bytes 73736 | tf_op jit(solution)/shard_map/ppermute | solution.py:78
  95.8 4.2 %collective-permute-start.2 = (bf16[2,2,1,1,1,48,128]{6,5,0,1,2,4,3:T(8,128)(2,1)S(1)}, bf16[2,2,1,1,1,48,128]{6,5,0,1,2,4,3:T(8,128)(2,1)S(1)}, u32[]{:S(2)}, u32[]{:S(2)}) collective-permute-start(bf16[2,2,1,1,1,48,128]{6,5,0,1,2,4,3:T(8,128)(2,1)S(1)} %maximum_select_fusion.4), channel_id=1, source_target_pairs={{0,4},{1,5},{2,6},{3,7},{4,0},{5,1},{6,2},{7,3},{8,12},{9,13},{10,... | collective-permute-start | bytes 147464 | tf_op jit(solution)/shard_map/ppermute | solution.py:78
  99.9 4.7 %collective-permute-start.3 = (bf16[2,2,2,1,1,48,128]{6,5,0,1,2,4,3:T(8,128)(2,1)S(1)}, bf16[2,2,2,1,1,48,128]{6,5,0,1,2,4,3:T(8,128)(2,1)S(1)}, u32[]{:S(2)}, u32[]{:S(2)}) collective-permute-start(bf16[2,2,2,1,1,48,128]{6,5,0,1,2,4,3:T(8,128)(2,1)S(1)} %maximum_select_fusion.2), channel_id=1, source_target_pairs={{0,1},{1,0},{2,3},{3,2},{4,5},{5,4},{6,7},{7,6},{8,9},{9,8},{10,11... | collective-permute-start | bytes 294920 | tf_op jit(solution)/shard_map/ppermute | solution.py:78
  104.6 1.5 collective-permute-start.4
  113.0 13.3 %slice-start.3 = ((s8[4718592]{0:T(1024)(128)(4,1)}), s8[524288]{0:T(1024)(128)(4,1)S(1)}, s32[]{:S(2)}) async-start(s8[4718592]{0:T(1024)(128)(4,1)} %bitcast.251), calls=%async_computation.3 | async-start | bytes 1048576
  116.4 37.0 %collective-permute-start.22 = (bf16[256,1536]{1,0:T(8,128)(2,1)}, bf16[256,1536]{1,0:T(8,128)(2,1)}, u32[]{:S(2)}, u32[]{:S(2)}) collective-permute-start(bf16[256,1536]{1,0:T(8,128)(2,1)} %get-tuple-element.36), channel_id=1, source_target_pairs={{0,2},{1,3},{2,0},{3,1},{4,6},{5,7},{6,4},{7,5},{8,10},{9,11},{10,... | collective-permute-start | bytes 2359304 | tf_op jit(solution)/shard_map/ppermute | solution.py:78
  129.4 45.1 %collective-permute-start.11 = (bf16[256,4608]{1,0:T(8,128)(2,1)}, bf16[256,4608]{1,0:T(8,128)(2,1)}, u32[]{:S(2)}, u32[]{:S(2)}) collective-permute-start(bf16[256,4608]{1,0:T(8,128)(2,1)} %pad_maximum_fusion.3), channel_id=1, source_target_pairs={{0,2},{1,3},{2,0},{3,1},{4,6},{5,7},{6,4},{7,5},{8,10},{9,11},{10,... | collective-permute-start | bytes 7077896 | tf_op jit(solution)/shard_map/ppermute | solution.py:78
  131.1 10.2 %copy-start.45 = (f32[1536]{0:T(1024)S(1)}, f32[1536]{0:T(1024)}, u32[]{:S(2)}) copy-start(f32[1536]{0:T(1024)} %get-tuple-element.32) | copy-start | bytes 18436
  142.6 5.8 %collective-permute-start.5 = (f32[78,128]{1,0:T(8,128)}, f32[78,128]{1,0:T(8,128)}, u32[]{:S(2)}, u32[]{:S(2)}) collective-permute-start(f32[78,128]{1,0:T(8,128)} %bitcast.18), channel_id=1, source_target_pairs={{0,1},{1,0},{2,3},{3,2},{4,5},{5,4},{6,7},{7,6},{8,9},{9,8},{10,11... | collective-permute-start | bytes 119816 | tf_op jit(solution)/shard_map/ppermute | solution.py:78
  149.2 1.3 collective-permute-start.6
  150.2 24.3 %collective-permute-start.10 = (bf16[384,256]{1,0:T(8,128)(2,1)}, bf16[384,256]{1,0:T(8,128)(2,1)}, u32[]{:S(2)}, u32[]{:S(2)}) collective-permute-start(bf16[384,256]{1,0:T(8,128)(2,1)} %get-tuple-element.67), channel_id=1, source_target_pairs={{0,2},{1,3},{2,0},{3,1},{4,6},{5,7},{6,4},{7,5},{8,10},{9,11},{10,... | collective-permute-start | bytes 589832 | tf_op jit(solution)/shard_map/ppermute | solution.py:78
  151.9 14.9 %collective-permute-start.7 = (f32[78,128]{1,0:T(8,128)}, f32[78,128]{1,0:T(8,128)}, u32[]{:S(2)}, u32[]{:S(2)}) collective-permute-start(f32[78,128]{1,0:T(8,128)} %fusion.242), channel_id=1, source_target_pairs={{0,4},{1,5},{2,6},{3,7},{4,0},{5,1},{6,2},{7,3},{8,12},{9,13},{10,... | collective-permute-start | bytes 119816 | tf_op jit(solution)/shard_map/ppermute | solution.py:78
  158.0 53.4 %collective-permute-start.23 = (bf16[768,1536]{1,0:T(8,128)(2,1)}, bf16[768,1536]{1,0:T(8,128)(2,1)}, u32[]{:S(2)}, u32[]{:S(2)}) collective-permute-start(bf16[768,1536]{1,0:T(8,128)(2,1)} %convolution_convert_fusion.2), channel_id=1, source_target_pairs={{0,1},{1,0},{2,3},{3,2},{4,5},{5,4},{6,7},{7,6},{8,9},{9,8},{10,11... | collective-permute-start | bytes 7077896 | tf_op jit(solution)/shard_map/ppermute | solution.py:78
  167.6 4.0 %collective-permute-start.8 = (f32[78,128]{1,0:T(8,128)S(1)}, f32[78,128]{1,0:T(8,128)S(1)}, u32[]{:S(2)}, u32[]{:S(2)}) collective-permute-start(f32[78,128]{1,0:T(8,128)S(1)} %add.387), channel_id=1, source_target_pairs={{0,8},{1,9},{2,10},{3,11},{4,12},{5,13},{6,14},{7,15},{8,0},{9,1},... | collective-permute-start | bytes 119816 | tf_op jit(solution)/shard_map/ppermute | solution.py:78
  169.3 10.5 %collective-permute-start.27 = (bf16[768,256]{1,0:T(8,128)(2,1)S(1)}, bf16[768,256]{1,0:T(8,128)(2,1)S(1)}, u32[]{:S(2)}, u32[]{:S(2)}) collective-permute-start(bf16[768,256]{1,0:T(8,128)(2,1)S(1)} %get-tuple-element.62), channel_id=1, source_target_pairs={{0,2},{1,3},{2,0},{3,1},{4,6},{5,7},{6,4},{7,5},{8,10},{9,11},{10,... | collective-permute-start | bytes 1179656 | tf_op jit(solution)/shard_map/ppermute | solution.py:78
  171.7 8.1 %collective-permute-start.9 = (f32[78,128]{1,0:T(8,128)S(1)}, f32[78,128]{1,0:T(8,128)S(1)}, u32[]{:S(2)}, u32[]{:S(2)}) collective-permute-start(f32[78,128]{1,0:T(8,128)S(1)} %add.388), channel_id=1, source_target_pairs={{0,16},{1,17},{2,18},{3,19},{4,20},{5,21},{6,22},{7,23},{8,24},{9,... | collective-permute-start | bytes 119816 | tf_op jit(solution)/shard_map/ppermute | solution.py:78
  177.6 40.5 %collective-permute-start.12 = (bf16[192,4608]{1,0:T(8,128)(2,1)S(1)}, bf16[192,4608]{1,0:T(8,128)(2,1)S(1)}, u32[]{:S(2)}, u32[]{:S(2)}) collective-permute-start(bf16[192,4608]{1,0:T(8,128)(2,1)S(1)} %convolution_convert_fusion), channel_id=1, source_target_pairs={{0,4},{1,5},{2,6},{3,7},{4,0},{5,1},{6,2},{7,3},{8,12},{9,13},{10,... | collective-permute-start | bytes 5308424 | tf_op jit(solution)/shard_map/ppermute | solution.py:78
  180.3 13.6 %collective-permute-start.29 = (bf16[384,768]{1,0:T(8,128)(2,1)S(1)}, bf16[384,768]{1,0:T(8,128)(2,1)S(1)}, u32[]{:S(2)}, u32[]{:S(2)}) collective-permute-start(bf16[384,768]{1,0:T(8,128)(2,1)S(1)} %convolution_convert_fusion.4), channel_id=1, source_target_pairs={{0,8},{1,9},{2,10},{3,11},{4,12},{5,13},{6,14},{7,15},{8,0},{9,1},... | collective-permute-start | bytes 1769480 | tf_op jit(solution)/shard_map/ppermute | solution.py:78
  194.1 27.5 %collective-permute-start.30 = (bf16[192,768]{1,0:T(8,128)(2,1)S(1)}, bf16[192,768]{1,0:T(8,128)(2,1)S(1)}, u32[]{:S(2)}, u32[]{:S(2)}) collective-permute-start(bf16[192,768]{1,0:T(8,128)(2,1)S(1)} %get-tuple-element.59), channel_id=1, source_target_pairs={{0,16},{1,17},{2,18},{3,19},{4,20},{5,21},{6,22},{7,23},{8,24},{9,... | collective-permute-start | bytes 884744 | tf_op jit(solution)/shard_map/ppermute | solution.py:78
  213.6 29.2 %collective-permute-start.24 = (bf16[384,1536]{1,0:T(8,128)(2,1)S(1)}, bf16[384,1536]{1,0:T(8,128)(2,1)S(1)}, u32[]{:S(2)}, u32[]{:S(2)}) collective-permute-start(bf16[384,1536]{1,0:T(8,128)(2,1)S(1)} %get-tuple-element.41), channel_id=1, source_target_pairs={{0,4},{1,5},{2,6},{3,7},{4,0},{5,1},{6,2},{7,3},{8,12},{9,13},{10,... | collective-permute-start | bytes 3538952 | tf_op jit(solution)/shard_map/ppermute | solution.py:78
  218.5 25.9 %collective-permute-start.13 = (bf16[96,4608]{1,0:T(8,128)(2,1)S(1)}, bf16[96,4608]{1,0:T(8,128)(2,1)S(1)}, u32[]{:S(2)}, u32[]{:S(2)}) collective-permute-start(bf16[96,4608]{1,0:T(8,128)(2,1)S(1)} %get-tuple-element.47), channel_id=1, source_target_pairs={{0,1},{1,0},{2,3},{3,2},{4,5},{5,4},{6,7},{7,6},{8,9},{9,8},{10,11... | collective-permute-start | bytes 2654216 | tf_op jit(solution)/shard_map/ppermute | solution.py:78
  221.6 17.9 %collective-permute-start.31 = (bf16[96,768]{1,0:T(8,128)(2,1)S(1)}, bf16[96,768]{1,0:T(8,128)(2,1)S(1)}, u32[]{:S(2)}, u32[]{:S(2)}) collective-permute-start(bf16[96,768]{1,0:T(8,128)(2,1)S(1)} %get-tuple-element.65), channel_id=1, source_target_pairs={{0,1},{1,0},{2,3},{3,2},{4,5},{5,4},{6,7},{7,6},{8,9},{9,8},{10,11... | collective-permute-start | bytes 442376 | tf_op jit(solution)/shard_map/ppermute | solution.py:78
  239.6 5.9 %collective-permute-start.32 = (bf16[48,768]{1,0:T(8,128)(2,1)S(1)}, bf16[48,768]{1,0:T(8,128)(2,1)S(1)}, u32[]{:S(2)}, u32[]{:S(2)}) collective-permute-start(bf16[48,768]{1,0:T(8,128)(2,1)S(1)} %dynamic-slice_add_fusion.18), channel_id=1, source_target_pairs={{0,4},{1,5},{2,6},{3,7},{4,0},{5,1},{6,2},{7,3},{8,12},{9,13},{10,... | collective-permute-start | bytes 221192 | tf_op jit(solution)/shard_map/ppermute | solution.py:78
  243.1 19.5 %collective-permute-start.25 = (bf16[192,1536]{1,0:T(8,128)(2,1)S(1)}, bf16[192,1536]{1,0:T(8,128)(2,1)S(1)}, u32[]{:S(2)}, u32[]{:S(2)}) collective-permute-start(bf16[192,1536]{1,0:T(8,128)(2,1)S(1)} %get-tuple-element.49), channel_id=1, source_target_pairs={{0,8},{1,9},{2,10},{3,11},{4,12},{5,13},{6,14},{7,15},{8,0},{9,1},... | collective-permute-start | bytes 1769480 | tf_op jit(solution)/shard_map/ppermute | solution.py:78
  244.6 25.9 %collective-permute-start.14 = (bf16[48,4608]{1,0:T(8,128)(2,1)S(1)}, bf16[48,4608]{1,0:T(8,128)(2,1)S(1)}, u32[]{:S(2)}, u32[]{:S(2)}) collective-permute-start(bf16[48,4608]{1,0:T(8,128)(2,1)S(1)} %get-tuple-element.51), channel_id=1, source_target_pairs={{0,8},{1,9},{2,10},{3,11},{4,12},{5,13},{6,14},{7,15},{8,0},{9,1},... | collective-permute-start | bytes 1327112 | tf_op jit(solution)/shard_map/ppermute | solution.py:78
  262.7 18.1 %collective-permute-start.26 = (bf16[96,1536]{1,0:T(8,128)(2,1)S(1)}, bf16[96,1536]{1,0:T(8,128)(2,1)S(1)}, u32[]{:S(2)}, u32[]{:S(2)}) collective-permute-start(bf16[96,1536]{1,0:T(8,128)(2,1)S(1)} %dynamic-slice_add_fusion.10), channel_id=1, source_target_pairs={{0,16},{1,17},{2,18},{3,19},{4,20},{5,21},{6,22},{7,23},{8,24},{9,... | collective-permute-start | bytes 884744 | tf_op jit(solution)/shard_map/ppermute | solution.py:78
  270.5 13.2 %collective-permute-start.15 = (bf16[24,4608]{1,0:T(8,128)(2,1)S(1)}, bf16[24,4608]{1,0:T(8,128)(2,1)S(1)}, u32[]{:S(2)}, u32[]{:S(2)}) collective-permute-start(bf16[24,4608]{1,0:T(8,128)(2,1)S(1)} %dynamic-slice_add_fusion.11), channel_id=1, source_target_pairs={{0,16},{1,17},{2,18},{3,19},{4,20},{5,21},{6,22},{7,23},{8,24},{9,... | collective-permute-start | bytes 663560 | tf_op jit(solution)/shard_map/ppermute | solution.py:78
  (43 other events, 175.6 us)

commit v2 on v1

v2 whole, which is shorter than its diff:
```python
import functools
import math

import jax
import jax.numpy as jnp
import numpy as np
from jax import lax
from jax.experimental import pallas as pl
from jax.experimental.pallas import tpu as pltpu
from jax.sharding import PartitionSpec as P

SEQ_LEN = 128
AXES = ("dp", "dir")
LANES = 128
MIB = 1 << 20

eps = 1e-05
root_half = 0.7071067811865476
inv_root_two_pi = 0.3989422804014327
bf16 = jnp.bfloat16
f32 = jnp.float32


def fourier(length):
    freq = np.arange(length)[:, None] + 0.5
    time = np.arange(length)[None, :]
    angle = np.pi * freq * time / length
    ahead = np.concatenate([np.cos(angle), -np.sin(angle)], axis=0)
    return ahead, ahead.T / length


def in_two(a):
    high = a.astype(np.float32).astype(jnp.bfloat16)
    low = (a - high.astype(np.float64)).astype(np.float32).astype(jnp.bfloat16)
    return high, low


def mm(a, b):
    return jnp.dot(a, b, preferred_element_type=f32)


def mm_t(a, b):
    return lax.dot_general(a, b, (((1,), (1,)), ((), ())), preferred_element_type=f32)


def spec(shape, index):
    return pl.BlockSpec(shape, index)


def in_hbm(*arrays):
    return [pltpu.with_memory_space_constraint(a, pltpu.HBM) for a in arrays]


def whole(shape):
    return pl.BlockSpec(shape, lambda *_: (0,) * len(shape))


def params(mib=56):
    return pltpu.CompilerParams(vmem_limit_bytes=mib * MIB)


def row(ref, first=0, count=None):
    count = ref.shape[0] if count is None else count
    return ref[pl.ds(first, count)].reshape(1, count)


BLOCK = 768


def took(us):
    return pl.CostEstimate(flops=int(us * 1e9), bytes_accessed=int(us * 3e6), transcendentals=0)


def sort_place(block, me, order):
    apart = block ^ me
    place = 0
    for b in order:
        place = place * 2 + ((apart >> b) & 1)
    return place


def sort_block(place, me, order):
    block = 0
    for k, b in enumerate(order):
        block = block | (((place >> (len(order) - 1 - k)) & 1) << b)
    return block ^ me


def rows_kernel(me, step, *rest):
    sources, (out, held, zs, sems) = rest[:4], rest[4:]
    i = pl.program_id(0)
    blocks = pl.num_programs(0)
    span = held.shape[-1]
    quarter = pl.multiple_of((me[0] & 3) * span, LANES)
    copies = [pltpu.make_async_copy(s.at[:, pl.ds(quarter, span)], held.at[k], sems.at[k]) for k, s in enumerate(sources)]

    @pl.when(i == 0)
    def _():
        for c in copies:
            c.start()
        for c in copies:
            c.wait()

    here = pl.multiple_of(i * LANES, LANES)
    decay, freq, real, imag = [held[k, :, pl.ds(here, LANES)] for k in range(4)]
    delta = jnp.exp(row(step, pl.multiple_of(quarter + here, LANES), LANES))
    rate = jnp.exp(decay)
    damp = jnp.exp(-rate * delta)
    angle = freq * delta
    zr, zi = damp * jnp.cos(angle), damp * jnp.sin(angle)
    for k in range(4):
        zs[2 * k], zs[2 * k + 1] = zr, zi
        zr, zi = zr * zr - zi * zi, 2.0 * zr * zi
    zs[8], zs[9] = real, imag
    zs[10], zs[11] = 2.0 * zs[6], zs[6] * zs[6] + zs[7] * zs[7]
    states = zs.shape[1]
    sub = lax.broadcasted_iota(jnp.int32, (8, LANES), 0)
    picks = [(sub >> k) % 2 == 1 for k in range(3)]
    count = SEQ_LEN // 8
    group = 4

    def body(step_no, accs):
        accs = list(accs)
        ys = []
        for u in range(group):
            n = step_no * group + u
            row = lambda k: jnp.broadcast_to(zs[k, pl.ds(n, 1), :], (8, LANES))
            wr, wi = row(8), row(9)
            for k in range(3):
                pr = jnp.where(picks[k], row(2 * k), 1.0)
                pi = jnp.where(picks[k], row(2 * k + 1), 0.0)
                wr, wi = wr * pr - wi * pi, wr * pi + wi * pr
            ys.append((wr, wr * row(6) - wi * row(7), row(10), row(11)))
        for a in range(count):
            accs[a] = accs[a] + ((ys[0][0] + ys[1][0]) + (ys[2][0] + ys[3][0]))
            if a < count - 1:
                ys = [(after, p * after - q * now, p, q) for now, after, p, q in ys]
        return tuple(accs)

    accs = lax.fori_loop(0, states // group, body, tuple(jnp.zeros((8, LANES), f32) for _ in range(count)))
    out[0] = (jnp.concatenate(accs, axis=0) * delta).astype(bf16)


def kernel_rows(me, step, decay_t, freq_t, real_t, imag_t):
    states, chans = decay_t.shape
    blocks = chans // 4 // LANES
    return pl.pallas_call(
        rows_kernel,
        grid_spec=pltpu.PrefetchScalarGridSpec(
            num_scalar_prefetch=1,
            grid=(blocks,),
            in_specs=[whole(step.shape)] + [pl.BlockSpec(memory_space=pltpu.HBM)] * 4,
            out_specs=spec((1, SEQ_LEN, LANES), lambda i, m: (i, 0, 0)),
            scratch_shapes=[
                pltpu.VMEM((4, states, chans // 4), f32),
                pltpu.VMEM((12, states, LANES), f32),
                pltpu.SemaphoreType.DMA((4,)),
            ],
        ),
        out_shape=jax.ShapeDtypeStruct((blocks, SEQ_LEN, LANES), bf16),
        compiler_params=params(8),
        cost_estimate=took(4),
        name="kernel_rows",
    )(me, step, *in_hbm(decay_t, freq_t, real_t, imag_t))


def gelu_both(v):
    size = jnp.abs(v)
    bell = jnp.exp(-0.5 * v * v)
    t = 1.0 / (1.0 + (0.3275911 * root_half) * size)
    poly = t * (0.127414796 + t * (-0.142248368 + t * (0.7107068705 + t * (-0.7265760135 + t * 0.5307027145))))
    tail = poly * bell
    phi = jnp.where(v >= 0.0, 1.0 - tail, tail)
    return v * phi, phi + (inv_root_two_pi * v) * bell


def norm_of(inputs):
    centered = inputs - jnp.mean(inputs, axis=1, keepdims=True)
    deviation = lax.rsqrt(jnp.mean(centered * centered, axis=1, keepdims=True) + eps)
    return centered * deviation, deviation


def scatter_blocks(source, me, order, first, own, send):
    size, half = own.shape[1], own.shape[0]
    for b in range(source.shape[0] // size):
        place = sort_place(first + b, me, order)
        block = source[b * size : (b + 1) * size]

        @pl.when(place < half)
        def _():
            own[place] = block

        @pl.when(place >= half)
        def _():
            send[place - half] = block


def project_kernel(
    counts, order, aligned, me, tokens, gain, bias, row_place, row_rest, up_b, val_b, gate_b, cot, up_hbm, val_hbm, out_hbm, gate_hbm,
    up_slope, val_act, val_slope, d_gated, gate_pre, low_own, low_send, *rest,
):
    *turned, normed, act, up_w, val_w, out_w, gate_w, sems = rest
    n_up, n_val, n_out, n_gate = counts
    block = BLOCK
    j = pl.program_id(0)
    per = gate_w.shape[0] // n_up

    copies = []
    for k in range(n_up):
        copies.append((up_hbm.at[:, pl.ds(k * block, block)], up_w.at[k]))
    for k in range(n_val):
        copies.append((val_hbm.at[:, pl.ds(k * block, block)], val_w.at[k]))
    for k in range(n_out):
        copies.append((out_hbm.at[pl.ds(k * block, block)], out_w.at[k]))
    for k in range(n_up):
        copies.append((gate_hbm.at[pl.ds(k * per, per)], gate_w.at[pl.ds(k * per, per)]))
    copies = [pltpu.make_async_copy(a, b, sems.at[i]) for i, (a, b) in enumerate(copies)]

    @pl.when(j == 0)
    def _():
        for c in copies:
            c.start()
        xhat, _ = norm_of(tokens[...].astype(f32))
        normed[...] = (xhat * row(gain) + row(bias)).astype(bf16)
        width = tokens.shape[1]
        lanes = sort_block(row_place[...], me[0], order) * per_block(width, order) + row_rest[...]
        pick = jnp.where(lax.broadcasted_iota(jnp.int32, (width, width), 0) == lanes, 1.0, 0.0).astype(bf16)
        sorted_rows = mm(normed[...], pick).T.astype(bf16)
        low_own[...] = sorted_rows[: width // 2]
        low_send[...] = sorted_rows[width // 2 :]

    for k in range(n_up):

        @pl.when(j == k)
        def _():
            copies[k].wait()

    @pl.when(j < n_up)
    def _():
        out, slope = gelu_both(mm(normed[...], up_w[j]) + row(up_b, pl.multiple_of(j * block, block), block))
        act[j] = out.astype(bf16)
        up_slope[...] = slope.astype(up_slope.dtype)
        flipped = out.T.astype(bf16)
        if aligned:
            own, send = turned
            scatter_blocks(flipped, me[0], order, j * (flipped.shape[0] // own.shape[1]), own, send)
        else:
            turned[0][...] = flipped

    at = n_up
    for k in range(n_val):

        @pl.when(j == at + k)
        def _():
            copies[n_up + k].wait()
            out, slope = gelu_both(mm(normed[...], val_w[k]) + row(val_b, k * block, block))
            val_act[...] = out.astype(bf16)
            val_slope[...] = slope.astype(val_slope.dtype)

    at += n_val
    for k in range(n_out):

        @pl.when(j == at + k)
        def _():
            copies[n_up + n_val + k].wait()
            d_gated[...] = mm_t(cot[...], out_w[k])

    at += n_out
    for k in range(n_gate):

        @pl.when(j == at + k)
        def _():
            if k == 0:
                for c in copies[n_up + n_val + n_out :]:
                    c.wait()
            columns = slice(k * block, (k + 1) * block)
            total = row(gate_b, k * block, block) + mm(act[0], gate_w[:per, columns])
            for i in range(1, n_up):
                total = total + mm(act[i], gate_w[i * per : (i + 1) * per, columns])
            gate_pre[...] = total


def per_block(width, order):
    return width >> len(order)


def project(me, order, vectors, tokens, cot, up_weight, value_weight, out_weight, gate_weight):
    rows, width = tokens.shape
    hidden, chans = gate_weight.shape
    n = 1 << len(order)
    block = BLOCK
    n_up, n_val = hidden // block, chans // block
    counts = (n_up, n_val, n_val, n_val)
    size = hidden // n
    aligned = size % 16 == 0
    clip = lambda j, first, count: jnp.clip(j - first, 0, count - 1)
    up_at = lambda j, m: (0, clip(j, 0, n_up))
    val_at = lambda j, m: (0, clip(j, n_up, n_val))
    out_at = lambda j, m: (0, clip(j, n_up + n_val, n_val))
    gate_at = lambda j, m: (0, clip(j, n_up + 2 * n_val, n_val))
    tall = (rows, block)
    shapes = [
        ((rows, hidden), bf16, spec(tall, up_at)),
        ((rows, chans), bf16, spec(tall, val_at)),
        ((rows, chans), bf16, spec(tall, val_at)),
        ((rows, chans), f32, spec(tall, out_at)),
        ((rows, chans), f32, spec(tall, gate_at)),
        ((width // 2, rows), bf16, whole((width // 2, rows))),
        ((width // 2, rows), bf16, whole((width // 2, rows))),
    ]
    if aligned:
        shapes += [((n // 2, size, rows), bf16, whole((n // 2, size, rows)))] * 2
    else:
        shapes += [((hidden, rows), bf16, spec((block, rows), lambda j, m: (clip(j, 0, n_up), 0)))]
    row_no = np.arange(width, dtype=np.int32)[None]
    anywhere = pl.BlockSpec(memory_space=pl.ANY)
    return pl.pallas_call(
        functools.partial(project_kernel, counts, order, aligned),
        grid_spec=pltpu.PrefetchScalarGridSpec(
            num_scalar_prefetch=1,
            grid=(sum(counts),),
            in_specs=[
                whole((rows, width)),
                whole((width,)),
                whole((width,)),
                whole((1, width)),
                whole((1, width)),
                whole((hidden,)),
                whole((chans,)),
                whole((chans,)),
                whole((rows, width)),
                anywhere,
                anywhere,
                anywhere,
                anywhere,
            ],
            out_specs=[s[2] for s in shapes],
            scratch_shapes=[
                pltpu.VMEM((rows, width), bf16),
                pltpu.VMEM((n_up, rows, block), bf16),
                pltpu.VMEM((n_up, width, block), bf16),
                pltpu.VMEM((n_val, width, block), bf16),
                pltpu.VMEM((n_val, block, width), bf16),
                pltpu.VMEM((hidden, chans), bf16),
                pltpu.SemaphoreType.DMA((2 * n_up + 2 * n_val,)),
            ],
        ),
        out_shape=[jax.ShapeDtypeStruct(s[0], s[1]) for s in shapes],
        compiler_params=params(44),
        cost_estimate=took(13),
        name="project",
    )(
        me, tokens, *vectors[:2], jnp.asarray(row_no // (width // n)), jnp.asarray(row_no % (width // n)), *vectors[2:], cot,
        *in_hbm(up_weight, value_weight, out_weight, gate_weight),
    )


def branch_kernel(
    seqs, order, aligned, me, gate_pre, d_gated, val, slope, kern_a, kern_b, skip, ahead, back,
    gated, d_gate, d_val, gate_sum, skip_sum, val_sum, *rest,
):
    *turned, flat, flat_kern = rest
    length = SEQ_LEN
    j = pl.program_id(0)
    block = val.shape[1]
    turn = jnp.where(j < pl.num_programs(0) // 2, 1.0, -1.0).astype(f32)

    def spectrum(a):
        return mm(ahead[...], jnp.concatenate([a, a], axis=0))

    def unspectrum(re, im):
        both = jnp.concatenate([re, im], axis=0)
        high = both.astype(bf16)
        low = (both - high.astype(f32)).astype(bf16)
        two = mm(back[...], high)
        return two[:length] + two[length:] + mm(back[:length], low)

    kern_hat = spectrum(jnp.concatenate([kern_a[0], kern_b[0]], axis=1))
    kr, ki = kern_hat[:length], kern_hat[length:] * turn
    direct = row(skip)
    gr, gi = 0.0, 0.0
    gate_total, skip_total, val_total = 0.0, 0.0, 0.0
    for s in range(seqs):
        rows = slice(s * length, (s + 1) * length)
        v = val[rows]
        v_wide = v.astype(f32)
        hat = spectrum(v)
        vr, vi = hat[:length], hat[length:]
        ssm = unspectrum(kr * vr - ki * vi, kr * vi + ki * vr) + direct * v_wide
        ssm = ssm.astype(bf16).astype(f32)
        g = gate_pre[rows]
        d = d_gated[rows]
        gated_wide = g * ssm
        gated[rows] = gated_wide.astype(bf16)
        flat[pl.ds(j * block, block), rows] = gated_wide.T.astype(bf16)
        dg = (d * ssm).astype(bf16)
        d_gate[rows] = dg
        gate_total = gate_total + jnp.sum(dg.astype(f32), axis=0, keepdims=True)
        ds = (d * g).astype(bf16)
        ds_wide = ds.astype(f32)
        skip_total = skip_total + jnp.sum(ds_wide * v_wide, axis=0, keepdims=True)
        hat = spectrum(ds)
        dr, di = hat[:length], hat[length:]
        back_val = unspectrum(kr * dr + ki * di, kr * di - ki * dr) + direct * ds_wide
        dv = (back_val.astype(bf16).astype(f32) * slope[rows].astype(f32)).astype(bf16)
        d_val[rows] = dv
        val_total = val_total + jnp.sum(dv.astype(f32), axis=0, keepdims=True)
        gr = gr + dr * vr + di * vi
        gi = gi + di * vr - dr * vi
    gate_sum[...] = gate_total
    skip_sum[...] = skip_total
    val_sum[...] = val_total
    flat_kern[pl.ds(j * block, block), :] = unspectrum(gr, gi * turn).T

    @pl.when(j == pl.num_programs(0) - 1)
    def _():
        if aligned:
            own, send, kern_own, kern_send = turned
            scatter_blocks(flat, me[0], order, 0, own, send)
            scatter_blocks(flat_kern, me[0], order, 0, kern_own, kern_send)
        else:
            turned[0][...] = flat[...]
            turned[1][...] = flat_kern[...]


def branch(me, order, skip, gate_pre, d_gated, val, slope, kern):
    rows, chans = val.shape
    n = 1 << len(order)
    seqs = rows // SEQ_LEN
    block = 2 * LANES
    steps = chans // block
    size = chans // n
    aligned = size % 16 == 0
    ahead, back = fourier(SEQ_LEN)
    ahead = jnp.asarray(np.concatenate(in_two(ahead), axis=1))
    back = jnp.asarray(np.concatenate(in_two(back), axis=0))
    tall = spec((rows, block), lambda j, m: (0, j))
    flat = spec((1, block), lambda j, m: (0, j))
    part = chans // 4 // LANES

    def kern_at(k, j, m):
        lane_block = 2 * j + k
        return ((lane_block // part) ^ (m[0] & 3)) * part + lane_block % part, 0, 0

    shapes = [((rows, chans), bf16, tall)] * 3 + [((1, chans), f32, flat)] * 3
    if aligned:
        shapes += [((n // 2, size, rows), bf16, whole((n // 2, size, rows)))] * 2
        shapes += [((n // 2, size, SEQ_LEN), f32, whole((n // 2, size, SEQ_LEN)))] * 2
    else:
        shapes += [((chans, rows), bf16, whole((chans, rows))), ((chans, SEQ_LEN), f32, whole((chans, SEQ_LEN)))]
    return pl.pallas_call(
        functools.partial(branch_kernel, seqs, order, aligned),
        grid_spec=pltpu.PrefetchScalarGridSpec(
            num_scalar_prefetch=1,
            grid=(steps,),
            in_specs=[
                tall,
                tall,
                tall,
                tall,
                spec((1, SEQ_LEN, LANES), functools.partial(kern_at, 0)),
                spec((1, SEQ_LEN, LANES), functools.partial(kern_at, 1)),
                spec((block,), lambda j, m: (j,)),
                whole(ahead.shape),
                whole(back.shape),
            ],
            out_specs=[s[2] for s in shapes],
            scratch_shapes=[pltpu.VMEM((chans, rows), bf16), pltpu.VMEM((chans, SEQ_LEN), f32)],
        ),
        out_shape=[jax.ShapeDtypeStruct(s[0], s[1]) for s in shapes],
        compiler_params=params(16),
        cost_estimate=took(8),
        name="branch",
    )(me, gate_pre, d_gated, val, slope, kern, kern, skip, ahead, back)


def back_kernel(
    d_gate, slope, d_val, tokens, cot, gain, gate_hbm, up_hbm, val_hbm, d_up, up_sum, grad, gain_sum, bias_sum, cot_sum,
    total, gate_w, up_w, val_w, sems,
):
    j = pl.program_id(0)
    steps, block = gate_w.shape[0], gate_w.shape[1]
    copies = []
    for k in range(steps):
        copies.append((gate_hbm.at[pl.ds(k * block, block)], gate_w.at[k]))
        copies.append((up_hbm.at[:, pl.ds(k * block, block)], up_w.at[k]))
    copies.append((val_hbm, val_w))
    copies = [pltpu.make_async_copy(a, b, sems.at[i]) for i, (a, b) in enumerate(copies)]

    @pl.when(j == 0)
    def _():
        for c in copies:
            c.start()

    for k in range(steps):

        @pl.when(j == k)
        def _():
            copies[2 * k].wait()
            copies[2 * k + 1].wait()

    d = (mm_t(d_gate[...], gate_w[j]) * slope[...].astype(f32)).astype(bf16)
    d_up[...] = d
    up_sum[...] = jnp.sum(d.astype(f32), axis=0, keepdims=True)
    more = mm_t(d, up_w[j])

    @pl.when(j == 0)
    def _():
        total[...] = more

    @pl.when(j > 0)
    def _():
        total[...] += more

    @pl.when(j == pl.num_programs(0) - 1)
    def _():
        copies[-1].wait()
        whole_grad = total[...] + mm_t(d_val[...], val_w[...])
        xhat, deviation = norm_of(tokens[...].astype(f32))
        gain_sum[...] = jnp.sum(whole_grad * xhat, axis=0, keepdims=True)
        bias_sum[...] = jnp.sum(whole_grad, axis=0, keepdims=True)
        e = whole_grad * row(gain)
        inner = e - jnp.mean(e, axis=1, keepdims=True) - xhat * jnp.mean(e * xhat, axis=1, keepdims=True)
        wide = cot[...].astype(f32)
        cot_sum[...] = jnp.sum(wide, axis=0, keepdims=True)
        grad[...] = (wide + deviation * inner).astype(bf16)


def back_through(gain, d_gate, slope, d_val, tokens, cot, gate_weight, up_weight, value_weight):
    rows, chans = d_gate.shape
    hidden, width = gate_weight.shape[0], tokens.shape[1]
    block = 512
    steps = hidden // block
    column = lambda j: (0, j)
    flat = whole((1, width))
    anywhere = pl.BlockSpec(memory_space=pl.ANY)
    return pl.pallas_call(
        back_kernel,
        grid=(steps,),
        in_specs=[
            whole((rows, chans)),
            spec((rows, block), column),
            whole((rows, chans)),
            whole((rows, width)),
            whole((rows, width)),
            whole((width,)),
            anywhere,
            anywhere,
            anywhere,
        ],
        out_specs=[spec((rows, block), column), spec((1, block), column), whole((rows, width)), flat, flat, flat],
        out_shape=[
            jax.ShapeDtypeStruct((rows, hidden), bf16),
            jax.ShapeDtypeStruct((1, hidden), f32),
            jax.ShapeDtypeStruct((rows, width), bf16),
        ]
        + [jax.ShapeDtypeStruct((1, width), f32)] * 3,
        scratch_shapes=[
            pltpu.VMEM((rows, width), f32),
            pltpu.VMEM((steps, block, chans), bf16),
            pltpu.VMEM((steps, width, block), bf16),
            pltpu.VMEM((width, chans), bf16),
            pltpu.SemaphoreType.DMA((2 * steps + 1,)),
        ],
        compiler_params=params(32),
        cost_estimate=took(1),
        name="back_through",
    )(d_gate, slope, d_val, tokens, cot, gain, *in_hbm(gate_weight, up_weight, value_weight))


def mixed_kernel(tokens, gated, out_w, bias, mixed):
    mixed[...] = (tokens[...].astype(f32) + mm(gated[...], out_w[...]) + row(bias)).astype(bf16)


def mixed_of(bias, tokens, gated, out_weight):
    rows, width = tokens.shape
    return pl.pallas_call(
        mixed_kernel,
        grid=(1,),
        in_specs=[whole(tokens.shape), whole(gated.shape), whole(out_weight.shape), whole((width,))],
        out_specs=whole(tokens.shape),
        out_shape=jax.ShapeDtypeStruct((rows, width), bf16),
        compiler_params=params(16),
        cost_estimate=took(3),
        name="mixed",
    )(tokens, gated, out_weight, bias)


def kept(shape, dtype=bf16):
    return pltpu.HBM(shape, dtype)


def beside(a, b):
    return jnp.concatenate([a[...], b[...]], axis=1)


def above(a, b):
    return jnp.concatenate([a[...], b[...]], axis=0)


def split_first(g, keep, send):
    half = g.shape[0] // 2
    keep[...] = g[:half]
    send[...] = g[half:]


def split_second(g, keep, send):
    quarter = g.shape[0] // 4
    keep[0] = g[:quarter]
    send[0] = g[quarter : 2 * quarter]
    keep[1] = g[2 * quarter : 3 * quarter]
    send[1] = g[3 * quarter :]


def gate_grad_kernel(lhs_a, lhs_b, rhs_a, rhs_b, keep1, send1, keep2, send2):
    j = pl.program_id(0)
    middle = pl.num_programs(0) // 2
    g = mm(beside(lhs_a, lhs_b), above(rhs_a, rhs_b)).astype(bf16)

    @pl.when(j < middle)
    def _():
        split_first(g, keep1, send1)

    @pl.when(j >= middle)
    def _():
        split_second(g, keep2, send2)


def gate_grad(lhs_a, lhs_b, rhs_a, rhs_b):
    rows, depth = lhs_a.shape
    cols = rhs_a.shape[1]
    block = 384
    steps = cols // block
    middle = steps // 2
    column = spec((depth, block), lambda j: (0, j))
    one = spec((rows // 2, block), lambda j: (0, jnp.minimum(j, middle - 1)))
    two = spec((2, rows // 4, block), lambda j: (0, 0, jnp.maximum(j - middle, 0)))
    return pl.pallas_call(
        gate_grad_kernel,
        grid=(steps,),
        in_specs=[whole((rows, depth))] * 2 + [column] * 2,
        out_specs=[one, one, two, two],
        out_shape=[kept((rows // 2, cols // 2)), jax.ShapeDtypeStruct((rows // 2, cols // 2), bf16)]
        + [kept((2, rows // 4, cols // 2)), jax.ShapeDtypeStruct((2, rows // 4, cols // 2), bf16)],
        compiler_params=params(16),
        cost_estimate=took(6),
        name="gate_grad",
    )(lhs_a, lhs_b, rhs_a, rhs_b)


def input_grad_kernel(n_up, lhs_a, lhs_b, up_a, up_b, val_a, val_b, keep1, send1, keep2, send2):
    j = pl.program_id(0)
    middle = pl.num_programs(0) // 2

    def write(a, b):
        g = mm(beside(lhs_a, lhs_b), above(a, b)).astype(bf16)

        @pl.when(j < middle)
        def _():
            split_first(g, keep1, send1)

        @pl.when(j >= middle)
        def _():
            split_second(g, keep2, send2)

    for use, a, b in ((j < n_up, up_a, up_b), (j >= n_up, val_a, val_b)):

        @pl.when(use)
        def _():
            write(a, b)


def input_grad(lhs_a, lhs_b, up_a, up_b, val_a, val_b, which):
    rows, depth = lhs_a.shape
    hidden, chans = up_a.shape[1], val_a.shape[1]
    cols = (hidden + chans) // 2
    block = 384
    steps, n_up, n_val = cols // block, hidden // block, chans // block
    first, middle = which * steps, steps // 2
    up = spec((depth, block), lambda j: (0, jnp.clip(first + j, 0, n_up - 1)))
    val = spec((depth, block), lambda j: (0, jnp.clip(first + j - n_up, 0, n_val - 1)))
    one = spec((rows // 2, block), lambda j: (0, jnp.minimum(j, middle - 1)))
    two = spec((2, rows // 4, block), lambda j: (0, 0, jnp.maximum(j - middle, 0)))
    return pl.pallas_call(
        functools.partial(input_grad_kernel, n_up - first),
        grid=(steps,),
        in_specs=[whole((rows, depth))] * 2 + [up, up, val, val],
        out_specs=[one, one, two, two],
        out_shape=[kept((rows // 2, cols // 2))] * 2 + [kept((2, rows // 4, cols // 2))] * 2,
        compiler_params=params(16),
        cost_estimate=took(60),
        name="input_grad",
    )(lhs_a, lhs_b, up_a, up_b, val_a, val_b)


def fold_kernel(last, *refs):
    pairs = 2 if len(refs) > 4 else 1
    ins, outs = refs[: 2 * pairs], refs[2 * pairs :]
    at = 0
    for p in range(pairs):
        total = ins[2 * p][...].astype(f32) + ins[2 * p + 1][...].astype(f32)
        columns = slice(at, at + total.shape[1])
        at += total.shape[1]
        if last:
            outs[0][:, columns] = total
        else:
            half = total.shape[0] // 2
            outs[0][:, columns] = total[:half]
            outs[1][:, columns] = total[half:].astype(bf16)


def fold(pairs, last=False, us=0.01):
    rows = pairs[0][0].shape[0]
    cols = sum(p[0].shape[1] for p in pairs)
    if rows % 32:
        total = jnp.concatenate([a.astype(f32) + b.astype(f32) for a, b in pairs], axis=1)
        return total if last else (total[: rows // 2], total[rows // 2 :].astype(bf16))
    if last:
        shapes = jax.ShapeDtypeStruct((rows, cols), f32)
    else:
        shapes = [jax.ShapeDtypeStruct((rows // 2, cols), f32), jax.ShapeDtypeStruct((rows // 2, cols), bf16)]
    return pl.pallas_call(
        functools.partial(fold_kernel, last),
        out_shape=shapes,
        compiler_params=params(16),
        cost_estimate=took(us),
        name="fold",
    )(*[a for p in pairs for a in p])


def pack_kernel(*refs):
    *vectors, out = refs
    at = 0
    for v in vectors:
        lines = v.shape[1] // LANES
        for k in range(lines):
            out[at + k : at + k + 1, :] = v[:, k * LANES : (k + 1) * LANES]
        at += lines


def pack(vectors):
    lines = sum(v.shape[1] for v in vectors) // LANES
    return pl.pallas_call(
        pack_kernel,
        out_shape=jax.ShapeDtypeStruct((lines, LANES), f32),
        compiler_params=params(8),
        cost_estimate=took(0.01),
        name="pack",
    )(*vectors)


def put_wide(wide, keep, send, cols):
    high = wide.astype(bf16)
    low = (wide - high.astype(f32)).astype(bf16)
    half, span = wide.shape[0] // 2, wide.shape[1]
    for part, ref in ((slice(0, half), keep), (slice(half, 2 * half), send)):
        ref[:, cols : cols + span] = high[part]
        ref[:, cols + span :] = low[part]


def out_grad_kernel(lhs_a, lhs_b, rhs_a, rhs_b, kern_a, kern_b, keep, send):
    g = mm(beside(lhs_a, lhs_b), above(rhs_a, rhs_b)).astype(bf16)
    half, cols = g.shape[0] // 2, g.shape[1]
    keep[:, :cols] = g[:half]
    send[:, :cols] = g[half:]
    put_wide(kern_a[...] + kern_b[...], keep, send, cols)


def out_grad(lhs_a, lhs_b, rhs_a, rhs_b, kern_a, kern_b):
    rows, depth = lhs_a.shape
    cols = rhs_a.shape[1] + 2 * kern_a.shape[1]
    return pl.pallas_call(
        out_grad_kernel,
        out_shape=[jax.ShapeDtypeStruct((rows // 2, cols), bf16)] * 2,
        compiler_params=params(16),
        cost_estimate=took(1),
        name="out_grad",
    )(lhs_a, lhs_b, rhs_a, rhs_b, kern_a, kern_b)


def out_add_kernel(cols, last, keep, recv, *outs):
    span = SEQ_LEN
    total = keep[:, :cols].astype(f32) + recv[:, :cols].astype(f32)
    wide = (keep[:, cols : cols + span].astype(f32) + keep[:, cols + span :].astype(f32)) + (
        recv[:, cols : cols + span].astype(f32) + recv[:, cols + span :].astype(f32)
    )
    if last:
        outs[0][...] = total
        outs[1][...] = wide
    else:
        half = total.shape[0] // 2
        outs[0][:, :cols] = total[:half].astype(bf16)
        outs[1][:, :cols] = total[half:].astype(bf16)
        put_wide(wide, *outs, cols)


def out_add(keep, recv, last):
    rows, every = keep.shape
    cols = every - 2 * SEQ_LEN
    if last:
        shapes = [jax.ShapeDtypeStruct((rows, cols), f32), jax.ShapeDtypeStruct((rows, SEQ_LEN), f32)]
    else:
        shapes = [jax.ShapeDtypeStruct((rows // 2, every), bf16)] * 2
    return pl.pallas_call(
        functools.partial(out_add_kernel, cols, last),
        out_shape=shapes,
        compiler_params=params(16),
        cost_estimate=took(0.01),
        name="out_add",
    )(keep, recv)


def param_kernel(me, grad, step, decay, freq, real, imag, g_step, g_decay, g_freq, g_real, g_imag, lags):
    own, chans = grad.shape[0], decay.shape[1]
    window = 2 * LANES
    first = me[0] * own
    start = pl.multiple_of(jnp.minimum(first // LANES * LANES, chans - window), LANES)

    def mine(ref):
        return pltpu.roll(ref[:, pl.ds(start, window)], window - (first - start), 1)[:, :own]

    delta = jnp.exp(pltpu.roll(jnp.broadcast_to(row(step, start, window), (8, window)), window - (first - start), 1)[:1, :own])
    rate, frequency, cr, ci = jnp.exp(mine(decay)), mine(freq), mine(real), mine(imag)
    damp = jnp.exp(-rate * delta)
    angle = frequency * delta
    zr, zi = damp * jnp.cos(angle), damp * jnp.sin(angle)
    lags[...] = grad[...].T
    zero = jnp.zeros_like(zr)

    def body(i, carry):
        pr, pi, dr, di = carry
        g = lags[pl.ds(SEQ_LEN - 1 - i, 1), :]
        dr, di = dr * zr - di * zi + pr, dr * zi + di * zr + pi
        pr, pi = pr * zr - pi * zi + g, pr * zi + pi * zr
        return pr, pi, dr, di

    pr, pi, dr, di = lax.fori_loop(0, SEQ_LEN, body, (zero, zero, zero, zero), unroll=4)
    sr, si = dr * zr - di * zi, dr * zi + di * zr
    ur, ui = cr * sr - ci * si, cr * si + ci * sr
    square = delta * delta
    g_real[...] = (delta * pr).T
    g_imag[...] = (-delta * pi).T
    g_freq[...] = (-square * ui).T
    g_decay[...] = (-square * rate * ur).T
    terms = delta * (cr * pr - ci * pi) - square * (rate * ur + frequency * ui)
    g_step[...] = jnp.sum(terms, axis=0, keepdims=True)


def param_grads(me, grad, step, decay_t, freq_t, real_t, imag_t):
    own, states = grad.shape[0], decay_t.shape[0]
    out = jax.ShapeDtypeStruct((own, states), f32)
    shapes = [jax.ShapeDtypeStruct((1, own), f32)] + [out] * 4
    args = (grad, step, decay_t, freq_t, real_t, imag_t)
    g = pl.pallas_call(
        param_kernel,
        grid_spec=pltpu.PrefetchScalarGridSpec(
            num_scalar_prefetch=1,
            grid=(1,),
            in_specs=[whole(a.shape) for a in args],
            out_specs=[whole(s.shape) for s in shapes],
            scratch_shapes=[pltpu.VMEM((SEQ_LEN, own), f32)],
        ),
        out_shape=shapes,
        compiler_params=params(16),
        cost_estimate=took(3.5),
        name="param_grads",
    )(me, *args)
    return g[0][0], *g[1:]


def local(
    n_dp,
    n_dir,
    tokens,
    layernorm_gain,
    layernorm_bias,
    up_weight,
    up_bias,
    value_weight,
    value_bias,
    step_log,
    decay_log,
    frequency,
    coef_real,
    coef_imag,
    skip_gain,
    gate_weight,
    gate_bias,
    out_weight,
    out_bias,
    cotangent,
):
    rows, width = tokens.shape
    chans = value_weight.shape[1]
    hidden = up_weight.shape[1]
    n = n_dp * n_dir
    nbits = int(math.log2(n))
    me = lax.axis_index("dp") * n_dir + lax.axis_index("dir")
    X, C, Y = 0, 1, 2
    rest = list(range(3, nbits))

    def swap(a, b):
        return lax.ppermute(a, AXES, [(j, j ^ (1 << b)) for j in range(n)])

    main_order = [C, X, Y] + rest
    out_order = [C] + rest + [X, Y]
    own_id = me[None]

    def sorted_halves(flat, order):
        every = jnp.arange(n, dtype=jnp.int32)
        blocks = flat.reshape(n, -1, flat.shape[1])[sort_block(every, me, order)]
        both = blocks.reshape(2, -1, flat.shape[1])
        return both[0], both[1]

    def after(value, *earlier):
        return lax.optimization_barrier((value, *earlier))[0]

    turned_params = [p.T for p in (decay_log, frequency, coef_real, coef_imag)]

    kern = kernel_rows(own_id, step_log, *turned_params)
    pair = jnp.concatenate([kern, swap(kern, C)], axis=0)
    across = swap(pair, X)
    part = kern.shape[0]

    cot_in = swap(cotangent, C)
    up_slope, value_act, value_slope, d_gated, gate_pre, norm_own, norm_send, *turned = project(
        own_id, main_order, (layernorm_gain, layernorm_bias, up_bias, value_bias, gate_bias), after(tokens, cot_in), cotangent, up_weight, value_weight, out_weight, gate_weight
    )
    if len(turned) == 2:
        act_own, act_send = [t.reshape(-1, rows) for t in turned]
    else:
        act_own, act_send = sorted_halves(turned[0], main_order)
    norm_in = swap(norm_send, C)
    act_in = swap(act_send, C)

    pair = after(pair, value_act)
    kern = jnp.concatenate([pair[:part], across[:part], pair[part:], across[part:]], axis=0)
    gated, d_gate, d_value, gate_sum, skip_sum, value_sum, *turned = branch(
        own_id, out_order, skip_gain, gate_pre, d_gated, value_act, value_slope, kern
    )
    if len(turned) == 4:
        gated_own, gated_send, kern_own, kern_send = [t.reshape(-1, t.shape[-1]) for t in turned]
    else:
        gated_own, gated_send = sorted_halves(turned[0], out_order)
        kern_own, kern_send = sorted_halves(turned[1], out_order)
    d_gate_in = swap(d_gate, C)
    gated_in = swap(gated_send, C)
    kern_in = swap(kern_send, C)
    d_value_in = swap(d_value, C)
    mixed = mixed_of(out_bias, tokens, gated, out_weight)

    keep1, send1, keep2, send2 = gate_grad(act_own, act_in, after(d_gate, mixed), d_gate_in)
    keep_o, send_o = out_grad(
        after(gated_own, send1, d_value_in, norm_in), gated_in, cotangent, cot_in, kern_own, kern_in
    )
    d_up, up_sum, grad_tokens, gain_sum, bias_sum, cot_sum = back_through(
        layernorm_gain, after(d_gate, send_o), up_slope, d_value, tokens, cotangent, gate_weight, up_weight, value_weight
    )
    d_up_in = swap(d_up, C)
    order = rest + [X, Y]

    last = [d_up]

    def then(value):
        return after(value, last[0])

    def done(*values):
        last[0] = values[0]
        return values if len(values) > 1 else values[0]

    def fold_next(pairs, final=False, us=0.01):
        first = (then(pairs[0][0]), pairs[0][1])
        result = fold([first] + pairs[1:], final, us)
        return done(result) if final else done(*result)

    def add_next(a, b):
        return done(then(a) + b)

    def out_next(keep, recv, final):
        return done(*out_add(then(keep), recv, final))

    def flat_rows(a):
        return a.reshape(-1, a.shape[-1])

    recv1, recv2, recv_o = swap(send1, X), swap(send2, Y), swap(send_o, order[0])
    keep_o, send_o = out_next(keep_o, recv_o, False)
    recv_o = swap(send_o, order[1])
    keep1, send1 = fold_next([(keep1, recv1)])
    recv1 = swap(send1, Y)
    keep2, send2 = fold_next([(flat_rows(keep2), flat_rows(recv2))], us=30)
    recv2 = swap(send2, X)
    keep1a, send1a, keep2a, send2a = done(*input_grad(norm_own, norm_in, then(d_up), d_up_in, d_value, d_value_in, 0))
    recv1a, recv2a = swap(send1a, X), swap(send2a, Y)
    keep1b, send1b, keep2b, send2b = done(*input_grad(norm_own, norm_in, then(d_up), d_up_in, d_value, d_value_in, 1))
    vectors = [gain_sum, bias_sum, cot_sum, up_sum, value_sum, gate_sum, skip_sum]
    packed = done(pack([then(vectors[0])] + vectors[1:]))
    packed_in = swap(packed, C)
    keep_o, send_o = out_next(keep_o, recv_o, False)
    packed = add_next(packed, packed_in)
    keep, send = fold_next([(keep1, recv1), (keep2, recv2)])
    recv = swap(send, rest[0])
    send1b, send2b = after(send1b, send), after(send2b, send)
    recv1b, recv2b = swap(send1b, X), swap(send2b, Y)
    keep1a, send1a = fold_next([(keep1a, recv1a)])
    recv1a = swap(send1a, Y)
    keep2a, send2a = fold_next([(flat_rows(keep2a), flat_rows(recv2a))])
    recv2a = swap(send2a, X)
    keep, send = fold_next([(keep, recv)])
    recv = swap(send, rest[1])
    keep1b, send1b = fold_next([(keep1b, recv1b)])
    recv1b = swap(send1b, Y)
    keep2b, send2b = fold_next([(flat_rows(keep2b), flat_rows(recv2b))])
    recv2b = swap(send2b, X)
    keep_a, send_a = fold_next([(keep1a, recv1a), (keep2a, recv2a)])
    recv_a = swap(send_a, rest[0])
    packed_in = swap(after(packed, send_a), X)
    recv_o = swap(after(send_o, send_a), order[2])
    keep_b, send_b = fold_next([(keep1b, recv1b), (keep2b, recv2b)])
    recv_b = swap(send_b, rest[0])
    packed = add_next(packed, packed_in)
    packed_in = swap(packed, Y)
    for b in rest[2:]:
        keep, send = fold_next([(keep, recv)])
        recv = swap(send, b)
    gate_share = fold_next([(keep, recv)], True)
    keep_a, send_a = fold_next([(keep_a, recv_a)])
    recv_a = swap(send_a, rest[1])
    for b in order[3:]:
        keep_o, send_o = out_next(keep_o, recv_o, False)
        recv_o = swap(send_o, b)
    packed = add_next(packed, packed_in)
    packed_in = swap(packed, rest[0])
    packed = add_next(packed, packed_in)
    packed_in = swap(packed, rest[1])
    keep_b, send_b = fold_next([(keep_b, recv_b)])
    recv_b = swap(after(send_b, packed), rest[1])
    for b in rest[2:]:
        keep_a, send_a = fold_next([(keep_a, recv_a)])
        recv_a = swap(send_a, b)
    out_share, grad_kern = out_next(keep_o, recv_o, True)
    share_a = fold_next([(keep_a, recv_a)], True)
    packed = add_next(packed, packed_in)
    for b in rest[2:]:
        packed = add_next(packed, swap(packed, b))
        keep_b, send_b = fold_next([(keep_b, recv_b)])
        recv_b = swap(send_b, b)
    share_b = fold_next([(keep_b, recv_b)], True)
    input_share = jnp.concatenate([share_a, share_b], axis=1)

    packed = packed.reshape(-1)
    sums, at = [], 0
    for v in vectors:
        sums.append(packed[at : at + v.shape[1]])
        at += v.shape[1]

    def share(v):
        size = v.shape[0] // n
        return lax.dynamic_slice_in_dim(v, me * size, size, 0)

    steps, decays, frequencies, reals, imags = param_grads(own_id, grad_kern, step_log, *turned_params)
    return (
        mixed,
        grad_tokens,
        sums[0],
        sums[1],
        input_share[:, :hidden],
        share(sums[3]),
        input_share[:, hidden:],
        share(sums[4]),
        steps,
        decays,
        frequencies,
        reals,
        imags,
        share(sums[6]),
        gate_share,
        share(sums[5]),
        out_share,
        sums[2],
    )


def solution(mesh):
    n_dp, n_dir = mesh.shape["dp"], mesh.shape["dir"]
    split, replicated = P(AXES), P()
    in_specs = (split,) + (replicated,) * 16 + (split,)
    out_specs = (split, split, replicated, replicated) + (split,) * 13 + (replicated,)

    def run(*args):
        return local(n_dp, n_dir, *args)

    return jax.shard_map(run, mesh=mesh, in_specs=in_specs, out_specs=out_specs, check_vma=False)
```

time: 291 us -> 150 us (0.52); the launches traced: 286 us -> 149 us
  waiting for transfers between devices: 103 us -> 40.5 us
  Pallas kernels: 0 us -> 62.3 us
  matrix products: 60.1 us -> 0 us
  local copies, waits for them, and re-layouts: 48.3 us -> 4.55 us
  other arithmetic: 36.3 us -> 0.99 us
  starting transfers between devices: 36.4 us -> 39.8 us
    pallas_call x0 -> x26, Pallas kernels: none -> 62.3 us  [the longest x1 13.6 us: project(): pl.pallas_call(functools.partial(project_kernel, counts, order, aligned),...]
    ppermute x33 -> x37, waiting for transfers between devices: 103 us -> 40.5 us  [swap(): return lax.ppermute(a, AXES, [(j, j ^ 1 << b) for j in range(n)])]
    dot_general x21 -> x0, matrix products: 60.1 us -> none  [the longest x1 11.7 us: local(): up_pre = jnp.dot(normed, up_weight, preferred_element_type=f32) + up_bias]
    unnamed x125 -> x60, local copies, waits for them, and re-layouts: 21.2 us -> 0.84 us
    reduce_sum x7 -> x0, other arithmetic: 15.6 us -> none  [the longest x1 9.83 us: kernel_rows(): coef_imag[:, :, None] * jnp.sin(phase)]
    add x22 -> x9, other arithmetic: 10.8 us -> 0.18 us  [the longest x4 0.15 us: fold(): a.astype(f32) + b.astype(f32)]
    transpose x4 -> x0, local copies, waits for them, and re-layouts: 7.04 us -> none  [the longest x3 5.12 us: ordered(): a = a.transpose(axes)]
    dynamic_slice x8 -> x0, local copies, waits for them, and re-layouts: 6.88 us -> none  [the longest x4 4.21 us: part(): return lax.dynamic_slice_in_dim(a, which * half, half, 0)]
  transfers between devices with their start and end apart: 33 -> 37, of which waited for: 18 -> 19; matrix products, arithmetic and copies ran while one was open for 47% -> 2% of each run, Pallas kernels for 0% -> 24%
where the time goes in v2:
time: 150 us; the launch traced here: 149 us
  Pallas kernels  62.3 us (42%)
  waiting for transfers between devices  40.5 us (27%)
  starting transfers between devices  39.8 us (27%)
  local copies, waits for them, and re-layouts  4.55 us (3%)
    ppermute x37, waiting for transfers between devices, swap(): return lax.ppermute(a, AXES, [(j, j ^ 1 << b) for j in range(n)])  40.5 us
    ppermute x37, starting transfers between devices, swap(): return lax.ppermute(a, AXES, [(j, j ^ 1 << b) for j in range(n)])  39.8 us
    pallas_call x1, Pallas kernels, project(): pl.pallas_call(functools.partial(project_kernel, counts, order, aligned),...  13.6 us
    pallas_call x1, Pallas kernels, back_through(): pl.pallas_call(back_kernel, grid=(steps,), in_specs=[whole((rows, chans))...  10.3 us
    pallas_call x2, Pallas kernels, input_grad(): pl.pallas_call(functools.partial(input_grad_kernel, n_up - first), grid=(...  8.56 us
    pallas_call x1, Pallas kernels, branch(): pl.pallas_call(functools.partial(branch_kernel, seqs, order, aligned), gr...  8.4 us
    pallas_call x1, Pallas kernels, gate_grad(): pl.pallas_call(gate_grad_kernel, grid=(steps,), in_specs=[whole((rows, de...  5.98 us
    pallas_call x1, Pallas kernels, kernel_rows(): pl.pallas_call(rows_kernel, grid_spec=pltpu.PrefetchScalarGridSpec(num_sc...  4.41 us
  transfers between devices with their start and end apart: 37, of which 19 were waited for; matrix products, arithmetic and copies ran while one was open for 2% of the time, Pallas kernels for 24%

profile of v2, /device:TPU:0, one launch (start us, length us, event | category | flops | bytes accessed | tf_op | source)
XLA Modules:
  0.0 149.3 jit_solution(11541263335259715263)
XLA Ops:
  0.7 0.7 copy-done.17
  1.4 4.4 %kernel_rows.1 = bf16[3,128,128]{2,1,0:T(8,128)(2,1)S(1)} custom-call(s32[1]{0:T(128)} %bitcast.me, f32[1536]{0:T(1024)S(1)} %copy-done.17, f32[64,1536]{1,0:T(8,128)} %bitcast.38, f32[64,1536]{1,0:T(8,128)} %bitcast.40, f32[64,1536]{1,0:T(8,128)} %bitcast.42, f32[64,1536]{1,0:T(8,128)} %bitcast.44), custom_call_target="tpu_custom_call" | custom-call | flops 4000000000 | bytes 12000000 | tf_op jit(solution)/shard_map/kernel_rows/pallas_call | solution.py:147
  6.4 0.9 collective-permute-done.1
  7.3 2.9 %collective-permute-start.2 = (bf16[6,128,128]{2,1,0:T(8,128)(2,1)S(1)}, bf16[6,128,128]{2,1,0:T(8,128)(2,1)S(1)}, u32[]{:S(2)}, u32[]{:S(2)}) collective-permute-start(bf16[6,128,128]{2,1,0:T(8,128)(2,1)S(1)} %pad_maximum_fusion.2), channel_id=1, source_target_pairs={{0,1},{1,0},{2,3},{3,2},{4,5},{5,4},{6,7},{7,6},{8,9},{9,8},{10,11... | collective-permute-start | bytes 589832 | tf_op jit(solution)/shard_map/ppermute | solution.py:903
  10.2 5.2 %collective-permute-done.2 = bf16[6,128,128]{2,1,0:T(8,128)(2,1)S(1)} collective-permute-done((bf16[6,128,128]{2,1,0:T(8,128)(2,1)S(1)}, bf16[6,128,128]{2,1,0:T(8,128)(2,1)S(1)}, u32[]{:S(2)}, u32[]{:S(2)}) %collective-permute-start.2) | collective-permute-done | bytes 196640 | tf_op jit(solution)/shard_map/ppermute | solution.py:903
  15.6 13.6 %project.1 = (bf16[256,3072]{1,0:T(8,128)(2,1)S(1)}, bf16[256,1536]{1,0:T(8,128)(2,1)S(1)}, bf16[256,1536]{1,0:T(8,128)(2,1)S(1)}, f32[256,1536]{1,0:T(8,128)S(1...) custom-call(s32[1]{0:T(128)} %bitcast.me, ...), custom_call_target="tpu_custom_call" | custom-call | flops 12999999488 | bytes 39000000 | tf_op jit(solution)/shard_map/project/pallas_call | solution.py:317
  29.3 8.4 %branch.1 = (bf16[256,1536]{1,0:T(8,128)(2,1)S(1)}, bf16[256,1536]{1,0:T(8,128)(2,1)S(1)}, bf16[256,1536]{1,0:T(8,128)(2,1)S(1)}, f32[1,1536]{1,0:T(1,128)S(1)},...) custom-call(s32[1]{0:T(128)} %bitcast.me, ...), custom_call_target="tpu_custom_call" | custom-call | flops 8000000000 | bytes 24000000 | tf_op jit(solution)/shard_map/branch/pallas_call | solution.py:451
  38.3 1.5 %mixed.1 = bf16[256,768]{1,0:T(8,128)(2,1)} custom-call(bf16[256,768]{1,0:T(8,128)(2,1)S(1)} %copy-done.5, bf16[256,1536]{1,0:T(8,128)(2,1)S(1)} %get-tuple-element.133.gated, bf16[1536,768]{1,0:T(8,128)(2,1)S(1)} %copy-done.8, f32[768]{0:T(1024)S(1)} %copy-done.20), custom_call_target="tpu_custom_call" | custom-call | flops 3000000000 | bytes 9000000 | tf_op jit(solution)/shard_map/mixed/pallas_call | solution.py:577
  41.2 6.0 %gate_grad.1 = (bf16[768,768]{1,0:T(8,128)(2,1)}, bf16[768,768]{1,0:T(8,128)(2,1)S(1)}, bf16[2,384,768]{2,1,0:T(8,128)(2,1)}, bf16[2,384,768]{2,1,0:T(8,128)(2,1)S(1)}) custom-call(bf16[1536,256]{1,0:T(8,128)(2,1)S(1)} %bitcast.49, bf16[1536,256]{1,0:T(8,128)(2,1)S(1)} %collective-permute-done.3.lhs_b, ...), custom_call_target="tpu_custom_call" | custom-call | flops 6000000000 | bytes 18000000 | tf_op jit(solution)/shard_map/gate_grad/pallas_call | solution.py:638
  47.2 1.7 %collective-permute-start.10 = (bf16[768,768]{1,0:T(8,128)(2,1)S(1)}, bf16[768,768]{1,0:T(8,128)(2,1)S(1)}, u32[]{:S(2)}, u32[]{:S(2)}) collective-permute-start(bf16[768,768]{1,0:T(8,128)(2,1)S(1)} %get-tuple-element.139), channel_id=1, source_target_pairs={{0,1},{1,0},{2,3},{3,2},{4,5},{5,4},{6,7},{7,6},{8,9},{9,8},{10,11... | collective-permute-start | bytes 3538952 | tf_op jit(solution)/shard_map/ppermute | solution.py:903
  48.9 1.5 %collective-permute-start.11 = (bf16[2,384,768]{2,1,0:T(8,128)(2,1)S(1)}, bf16[2,384,768]{2,1,0:T(8,128)(2,1)S(1)}, u32[]{:S(2)}, u32[]{:S(2)}) collective-permute-start(bf16[2,384,768]{2,1,0:T(8,128)(2,1)S(1)} %get-tuple-element.161), channel_id=1, source_target_pairs={{0,4},{1,5},{2,6},{3,7},{4,0},{5,1},{6,2},{7,3},{8,12},{9,13},{10,... | collective-permute-start | bytes 3538952 | tf_op jit(solution)/shard_map/ppermute | solution.py:903
  50.4 0.9 out_grad.1
  51.4 1.6 %collective-permute-start.9 = (bf16[384,1024]{1,0:T(8,128)(2,1)S(1)}, bf16[384,1024]{1,0:T(8,128)(2,1)S(1)}, u32[]{:S(2)}, u32[]{:S(2)}) collective-permute-start(bf16[384,1024]{1,0:T(8,128)(2,1)S(1)} %get-tuple-element.146), channel_id=1, source_target_pairs={{0,8},{1,9},{2,10},{3,11},{4,12},{5,13},{6,14},{7,15},{8,0},{9,1},... | collective-permute-start | bytes 2359304 | tf_op jit(solution)/shard_map/ppermute | solution.py:903
  53.0 10.3 %back_through.1 = (bf16[256,3072]{1,0:T(8,128)(2,1)S(1)}, f32[1,3072]{1,0:T(1,128)S(1)}, bf16[256,768]{1,0:T(8,128)(2,1)}, f32[1,768]{1,0:T(1,128)S(1)}, f32[1,768]{1,0:T(1,128)S(1)}, /*index=5*/f32[1,768]{1,0:T(1,128)S(1)}) custom-call(bf16[256,1536]{1,0:T(8,128)(2,1)S(1)} %get-tuple-element.147.rhs_a.d_gate, ...), custom_call_target="tpu_custom_call" | custom-call | flops 1000000000 | bytes 3000000 | tf_op jit(solution)/shard_map/back_through/pallas_call | solution.py:537
  63.4 7.0 %collective-permute-done.9.recv = bf16[384,1024]{1,0:T(8,128)(2,1)S(1)} collective-permute-done((bf16[384,1024]{1,0:T(8,128)(2,1)S(1)}, bf16[384,1024]{1,0:T(8,128)(2,1)S(1)}, u32[]{:S(2)}, u32[]{:S(2)}) %collective-permute-start.9) | collective-permute-done | bytes 786464 | tf_op jit(solution)/shard_map/ppermute | solution.py:903
  70.4 0.9 out_add.4
  71.3 2.6 %collective-permute-start.13 = (bf16[192,1024]{1,0:T(8,128)(2,1)}, bf16[192,1024]{1,0:T(8,128)(2,1)}, u32[]{:S(2)}, u32[]{:S(2)}) collective-permute-start(bf16[192,1024]{1,0:T(8,128)(2,1)} %get-tuple-element.175), channel_id=1, source_target_pairs={{0,16},{1,17},{2,18},{3,19},{4,20},{5,21},{6,22},{7,23},{8,24},{9,... | collective-permute-start | bytes 1179656 | tf_op jit(solution)/shard_map/ppermute | solution.py:903
  73.9 1.2 collective-permute-done.10.refs_1_
  75.5 1.1 collective-permute-done.11
  77.6 1.5 %collective-permute-start.15 = (bf16[384,768]{1,0:T(8,128)(2,1)S(1)}, bf16[384,768]{1,0:T(8,128)(2,1)S(1)}, u32[]{:S(2)}, u32[]{:S(2)}) collective-permute-start(bf16[384,768]{1,0:T(8,128)(2,1)S(1)} %get-tuple-element.179), channel_id=1, source_target_pairs={{0,4},{1,5},{2,6},{3,7},{4,0},{5,1},{6,2},{7,3},{8,12},{9,13},{10,... | collective-permute-start | bytes 1769480 | tf_op jit(solution)/shard_map/ppermute | solution.py:903
  79.1 4.3 %input_grad.2 = (bf16[192,1152]{1,0:T(8,128)(2,1)}, bf16[192,1152]{1,0:T(8,128)(2,1)}, bf16[2,96,1152]{2,1,0:T(8,128)(2,1)}, bf16[2,96,1152]{2,1,0:T(8,128)(2,1)}) custom-call(bf16[384,256]{1,0:T(8,128)(2,1)S(1)} %get-tuple-element.151.lhs_a, bf16[384,256]{1,0:T(8,128)(2,1)S(1)} %collective-permute-done.6.lhs_b, ...), custom_call_target="tpu_custom_call" | custom-call | flops 60000002048 | bytes 180000000 | tf_op jit(solution)/shard_map/input_grad/pallas_call | solution.py:684
  83.4 4.2 %input_grad.3 = (bf16[192,1152]{1,0:T(8,128)(2,1)}, bf16[192,1152]{1,0:T(8,128)(2,1)}, bf16[2,96,1152]{2,1,0:T(8,128)(2,1)}, bf16[2,96,1152]{2,1,0:T(8,128)(2,1)}) custom-call(bf16[384,256]{1,0:T(8,128)(2,1)S(1)} %get-tuple-element.151.lhs_a, bf16[384,256]{1,0:T(8,128)(2,1)S(1)} %collective-permute-done.6.lhs_b, ...), custom_call_target="tpu_custom_call" | custom-call | flops 60000002048 | bytes 180000000 | tf_op jit(solution)/shard_map/input_grad/pallas_call | solution.py:684
  87.7 2.9 %collective-permute-done.13.recv = bf16[192,1024]{1,0:T(8,128)(2,1)} collective-permute-done((bf16[192,1024]{1,0:T(8,128)(2,1)}, bf16[192,1024]{1,0:T(8,128)(2,1)}, u32[]{:S(2)}, u32[]{:S(2)}) %collective-permute-start.13) | collective-permute-done | bytes 393248 | tf_op jit(solution)/shard_map/ppermute | solution.py:903
  90.7 1.1 out_add.5
  93.1 0.8 collective-permute-start.19
  93.9 1.5 %collective-permute-start.20 = (bf16[192,1152]{1,0:T(8,128)(2,1)S(1)}, bf16[192,1152]{1,0:T(8,128)(2,1)S(1)}, u32[]{:S(2)}, u32[]{:S(2)}) collective-permute-start(bf16[192,1152]{1,0:T(8,128)(2,1)S(1)} %copy-done.27), channel_id=1, source_target_pairs={{0,1},{1,0},{2,3},{3,2},{4,5},{5,4},{6,7},{7,6},{8,9},{9,8},{10,11... | collective-permute-start | bytes 1327112 | tf_op jit(solution)/shard_map/ppermute | solution.py:903
  95.4 1.5 %collective-permute-start.21 = (bf16[2,96,1152]{2,1,0:T(8,128)(2,1)S(1)}, bf16[2,96,1152]{2,1,0:T(8,128)(2,1)S(1)}, u32[]{:S(2)}, u32[]{:S(2)}) collective-permute-start(bf16[2,96,1152]{2,1,0:T(8,128)(2,1)S(1)} %copy-done.26), channel_id=1, source_target_pairs={{0,4},{1,5},{2,6},{3,7},{4,0},{5,1},{6,2},{7,3},{8,12},{9,13},{10,... | collective-permute-start | bytes 1327112 | tf_op jit(solution)/shard_map/ppermute | solution.py:903
  96.9 8.0 %collective-permute-done.17.refs_1_ = bf16[192,1152]{1,0:T(8,128)(2,1)S(1)} collective-permute-done((bf16[192,1152]{1,0:T(8,128)(2,1)S(1)}, bf16[192,1152]{1,0:T(8,128)(2,1)S(1)}, u32[]{:S(2)}, u32[]{:S(2)}) %collective-permute-start.17) | collective-permute-done | bytes 442400 | tf_op jit(solution)/shard_map/ppermute | solution.py:903
  105.6 1.6 %collective-permute-start.23 = (bf16[96,1152]{1,0:T(8,128)(2,1)S(1)}, bf16[96,1152]{1,0:T(8,128)(2,1)S(1)}, u32[]{:S(2)}, u32[]{:S(2)}) collective-permute-start(bf16[96,1152]{1,0:T(8,128)(2,1)S(1)} %get-tuple-element.203), channel_id=1, source_target_pairs={{0,1},{1,0},{2,3},{3,2},{4,5},{5,4},{6,7},{7,6},{8,9},{9,8},{10,11... | collective-permute-start | bytes 663560 | tf_op jit(solution)/shard_map/ppermute | solution.py:903
  107.8 2.6 %collective-permute-start.27 = (bf16[96,1536]{1,0:T(8,128)(2,1)S(1)}, bf16[96,1536]{1,0:T(8,128)(2,1)S(1)}, u32[]{:S(2)}, u32[]{:S(2)}) collective-permute-start(bf16[96,1536]{1,0:T(8,128)(2,1)S(1)} %get-tuple-element.213), channel_id=1, source_target_pairs={{0,16},{1,17},{2,18},{3,19},{4,20},{5,21},{6,22},{7,23},{8,24},{9,... | collective-permute-start | bytes 884744 | tf_op jit(solution)/shard_map/ppermute | solution.py:903
  110.4 4.0 %collective-permute-done.20.refs_1_ = bf16[192,1152]{1,0:T(8,128)(2,1)S(1)} collective-permute-done((bf16[192,1152]{1,0:T(8,128)(2,1)S(1)}, bf16[192,1152]{1,0:T(8,128)(2,1)S(1)}, u32[]{:S(2)}, u32[]{:S(2)}) %collective-permute-start.20) | collective-permute-done | bytes 442400 | tf_op jit(solution)/shard_map/ppermute | solution.py:903
  115.1 1.6 %collective-permute-start.25 = (bf16[96,1152]{1,0:T(8,128)(2,1)S(1)}, bf16[96,1152]{1,0:T(8,128)(2,1)S(1)}, u32[]{:S(2)}, u32[]{:S(2)}) collective-permute-start(bf16[96,1152]{1,0:T(8,128)(2,1)S(1)} %get-tuple-element.207), channel_id=1, source_target_pairs={{0,1},{1,0},{2,3},{3,2},{4,5},{5,4},{6,7},{7,6},{8,9},{9,8},{10,11... | collective-permute-start | bytes 663560 | tf_op jit(solution)/shard_map/ppermute | solution.py:903
  117.1 2.0 %collective-permute-done.23.refs_3_ = bf16[96,1152]{1,0:T(8,128)(2,1)S(1)} collective-permute-done((bf16[96,1152]{1,0:T(8,128)(2,1)S(1)}, bf16[96,1152]{1,0:T(8,128)(2,1)S(1)}, u32[]{:S(2)}, u32[]{:S(2)}) %collective-permute-start.23) | collective-permute-done | bytes 221216 | tf_op jit(solution)/shard_map/ppermute | solution.py:903
  119.8 0.7 collective-permute-start.28
  120.5 1.5 collective-permute-start.26
  122.2 0.9 collective-permute-start.29
  123.3 1.7 %collective-permute-done.26 = f32[78,128]{1,0:T(8,128)S(1)} collective-permute-done((f32[78,128]{1,0:T(8,128)S(1)}, f32[78,128]{1,0:T(8,128)S(1)}, u32[]{:S(2)}, u32[]{:S(2)}) %collective-permute-start.26) | collective-permute-done | bytes 39968 | tf_op jit(solution)/shard_map/ppermute | solution.py:903
  125.5 1.2 collective-permute-start.32
  126.7 0.9 fold.21
  129.0 1.4 collective-permute-start.31
  130.8 3.0 %collective-permute-start.34 = (bf16[24,2304]{1,0:T(8,128)(2,1)S(1)}, bf16[24,2304]{1,0:T(8,128)(2,1)S(1)}, u32[]{:S(2)}, u32[]{:S(2)}) collective-permute-start(bf16[24,2304]{1,0:T(8,128)(2,1)S(1)} %slice.122), channel_id=1, source_target_pairs={{0,16},{1,17},{2,18},{3,19},{4,20},{5,21},{6,22},{7,23},{8,24},{9,... | collective-permute-start | bytes 331784 | tf_op jit(solution)/shard_map/ppermute | solution.py:903
  133.9 2.5 %collective-permute-start.35 = (f32[78,128]{1,0:T(8,128)S(1)}, f32[78,128]{1,0:T(8,128)S(1)}, u32[]{:S(2)}, u32[]{:S(2)}) collective-permute-start(f32[78,128]{1,0:T(8,128)S(1)} %add.43), channel_id=1, source_target_pairs={{0,16},{1,17},{2,18},{3,19},{4,20},{5,21},{6,22},{7,23},{8,24},{9,... | collective-permute-start | bytes 119816 | tf_op jit(solution)/shard_map/ppermute | solution.py:903
  136.4 0.7 out_add.7
  137.1 2.3 %collective-permute-done.34 = bf16[24,2304]{1,0:T(8,128)(2,1)S(1)} collective-permute-done((bf16[24,2304]{1,0:T(8,128)(2,1)S(1)}, bf16[24,2304]{1,0:T(8,128)(2,1)S(1)}, u32[]{:S(2)}, u32[]{:S(2)}) %collective-permute-start.34) | collective-permute-done | bytes 110624 | tf_op jit(solution)/shard_map/ppermute | solution.py:903
  139.4 0.8 collective-permute-done.35
  140.3 1.1 collective-permute-start.36
  141.4 3.6 %param_grads.1 = (f32[1,48]{1,0:T(1,128)}, f32[48,64]{1,0:T(8,128)}, f32[48,64]{1,0:T(8,128)}, f32[48,64]{1,0:T(8,128)}, f32[48,64]{1,0:T(8,128)}) custom-call(s32[1]{0:T(128)} %bitcast.me, f32[48,128]{1,0:T(8,128)S(1)} %get-tuple-element.230.grad, f32[1536]{0:T(1024)S(1)} %copy-done.18, f32[64,1536]{1,0:T(8,128)S(1)} %bitcast.39, f32[64,1536]{1,0:T(8,128)S(1)} %bitcast.41, ...), custom_call_target="tpu_custom_call" | custom-call | flops 3500000000 | bytes 10500000 | tf_op jit(solution)/shard_map/param_grads/pallas_call | solution.py:854
  147.9 0.7 pad_maximum_fusion.1
  (138 shorter events, 14.8 us)
Async XLA Ops:
  1.4 14.2 %copy-start.5 = (bf16[256,768]{1,0:T(8,128)(2,1)S(1)}, bf16[256,768]{1,0:T(8,128)(2,1)}, u32[]{:S(2)}) copy-start(bf16[256,768]{1,0:T(8,128)(2,1)} %tokens.4) | copy-start | bytes 1179652
  1.4 14.2 %copy-start.7 = (f32[768]{0:T(1024)S(1)}, f32[768]{0:T(1024)}, u32[]{:S(2)}) copy-start(f32[768]{0:T(1024)} %gain.3) | copy-start | bytes 9220
  1.4 14.2 %copy-start.13 = (f32[3072]{0:T(1024)S(1)}, f32[3072]{0:T(1024)}, u32[]{:S(2)}) copy-start(f32[3072]{0:T(1024)} %up_b.1) | copy-start | bytes 36868
  1.4 14.2 %copy-start.14 = (f32[1536]{0:T(1024)S(1)}, f32[1536]{0:T(1024)}, u32[]{:S(2)}) copy-start(f32[1536]{0:T(1024)} %val_b.1) | copy-start | bytes 18436
  1.4 14.2 %copy-start.15 = (f32[1536]{0:T(1024)S(1)}, f32[1536]{0:T(1024)}, u32[]{:S(2)}) copy-start(f32[1536]{0:T(1024)} %gate_b.1) | copy-start | bytes 18436
  1.4 14.2 %copy-start.19 = (f32[768]{0:T(1024)S(1)}, f32[768]{0:T(1024)}, u32[]{:S(2)}) copy-start(f32[768]{0:T(1024)} %bias.2) | copy-start | bytes 9220
  1.4 14.2 %copy-start.24 = (s32[1,768]{1,0:T(1,128)S(1)}, s32[1,768]{1,0:T(1,128)}, u32[]{:S(2)}) copy-start(s32[1,768]{1,0:T(1,128)} %constant.28.clone.row_place) | copy-start | bytes 9220
  1.4 14.2 %copy-start.25 = (s32[1,768]{1,0:T(1,128)S(1)}, s32[1,768]{1,0:T(1,128)}, u32[]{:S(2)}) copy-start(s32[1,768]{1,0:T(1,128)} %constant.29.clone.row_rest) | copy-start | bytes 9220
  5.8 1.5 collective-permute-start.1
  7.3 8.1 %collective-permute-start.2 = (bf16[6,128,128]{2,1,0:T(8,128)(2,1)S(1)}, bf16[6,128,128]{2,1,0:T(8,128)(2,1)S(1)}, u32[]{:S(2)}, u32[]{:S(2)}) collective-permute-start(bf16[6,128,128]{2,1,0:T(8,128)(2,1)S(1)} %pad_maximum_fusion.2), channel_id=1, source_target_pairs={{0,1},{1,0},{2,3},{3,2},{4,5},{5,4},{6,7},{7,6},{8,9},{9,8},{10,11... | collective-permute-start | bytes 589832 | tf_op jit(solution)/shard_map/ppermute | solution.py:903
  10.2 5.3 %collective-permute-start = (bf16[256,768]{1,0:T(8,128)(2,1)S(1)}, bf16[256,768]{1,0:T(8,128)(2,1)S(1)}, u32[]{:S(2)}, u32[]{:S(2)}) collective-permute-start(bf16[256,768]{1,0:T(8,128)(2,1)S(1)} %copy-done.6), channel_id=1, source_target_pairs={{0,2},{1,3},{2,0},{3,1},{4,6},{5,7},{6,4},{7,5},{8,10},{9,11},{10,... | collective-permute-start | bytes 1179656 | tf_op jit(solution)/shard_map/ppermute | solution.py:903
  15.5 13.8 %copy-start.16 = (f32[1536]{0:T(1024)S(1)}, f32[1536]{0:T(1024)}, u32[]{:S(2)}) copy-start(f32[1536]{0:T(1024)} %skip.1) | copy-start | bytes 18436
  15.5 13.8 %copy-start.22 = (bf16[256,256]{1,0:T(8,128)(2,1)S(1)}, bf16[256,256]{1,0:T(8,128)(2,1)}, u32[]{:S(2)}) copy-start(bf16[256,256]{1,0:T(8,128)(2,1)} %constant.30.clone.ahead) | copy-start | bytes 393220
  37.7 2.7 %collective-permute-start.4 = (bf16[256,1536]{1,0:T(8,128)(2,1)S(1)}, bf16[256,1536]{1,0:T(8,128)(2,1)S(1)}, u32[]{:S(2)}, u32[]{:S(2)}) collective-permute-start(bf16[256,1536]{1,0:T(8,128)(2,1)S(1)} %get-tuple-element.147.rhs_a.d_gate), channel_id=1, source_target_pairs={{0,2},{1,3},{2,0},{3,1},{4,6},{5,7},{6,4},{7,5},{8,10},{9,11},{10,... | collective-permute-start | bytes 2359304 | tf_op jit(solution)/shard_map/ppermute | solution.py:903
  37.8 3.4 %collective-permute-start.3 = (bf16[1536,256]{1,0:T(8,128)(2,1)S(1)}, bf16[1536,256]{1,0:T(8,128)(2,1)S(1)}, u32[]{:S(2)}, u32[]{:S(2)}) collective-permute-start(bf16[1536,256]{1,0:T(8,128)(2,1)S(1)} %bitcast.37), channel_id=1, source_target_pairs={{0,2},{1,3},{2,0},{3,1},{4,6},{5,7},{6,4},{7,5},{8,10},{9,11},{10,... | collective-permute-start | bytes 2359304 | tf_op jit(solution)/shard_map/ppermute | solution.py:903
  39.8 10.6 %collective-permute-start.5 = (bf16[256,1536]{1,0:T(8,128)(2,1)S(1)}, bf16[256,1536]{1,0:T(8,128)(2,1)S(1)}, u32[]{:S(2)}, u32[]{:S(2)}) collective-permute-start(bf16[256,1536]{1,0:T(8,128)(2,1)S(1)} %get-tuple-element.140.d_val.val_a), channel_id=1, source_target_pairs={{0,2},{1,3},{2,0},{3,1},{4,6},{5,7},{6,4},{7,5},{8,10},{9,11},{10,... | collective-permute-start | bytes 2359304 | tf_op jit(solution)/shard_map/ppermute | solution.py:903
  39.9 9.0 %collective-permute-start.6 = (bf16[384,256]{1,0:T(8,128)(2,1)S(1)}, bf16[384,256]{1,0:T(8,128)(2,1)S(1)}, u32[]{:S(2)}, u32[]{:S(2)}) collective-permute-start(bf16[384,256]{1,0:T(8,128)(2,1)S(1)} %get-tuple-element.141), channel_id=1, source_target_pairs={{0,2},{1,3},{2,0},{3,1},{4,6},{5,7},{6,4},{7,5},{8,10},{9,11},{10,... | collective-permute-start | bytes 589832 | tf_op jit(solution)/shard_map/ppermute | solution.py:903
  40.3 10.1 %collective-permute-start.7 = (bf16[768,256]{1,0:T(8,128)(2,1)S(1)}, bf16[768,256]{1,0:T(8,128)(2,1)S(1)}, u32[]{:S(2)}, u32[]{:S(2)}) collective-permute-start(bf16[768,256]{1,0:T(8,128)(2,1)S(1)} %bitcast.47), channel_id=1, source_target_pairs={{0,2},{1,3},{2,0},{3,1},{4,6},{5,7},{6,4},{7,5},{8,10},{9,11},{10,... | collective-permute-start | bytes 1179656 | tf_op jit(solution)/shard_map/ppermute | solution.py:903
  40.4 10.0 %collective-permute-start.8 = (f32[768,128]{1,0:T(8,128)S(1)}, f32[768,128]{1,0:T(8,128)S(1)}, u32[]{:S(2)}, u32[]{:S(2)}) collective-permute-start(f32[768,128]{1,0:T(8,128)S(1)} %bitcast.46), channel_id=1, source_target_pairs={{0,2},{1,3},{2,0},{3,1},{4,6},{5,7},{6,4},{7,5},{8,10},{9,11},{10,... | collective-permute-start | bytes 1179656 | tf_op jit(solution)/shard_map/ppermute | solution.py:903
  47.2 28.0 %collective-permute-start.10 = (bf16[768,768]{1,0:T(8,128)(2,1)S(1)}, bf16[768,768]{1,0:T(8,128)(2,1)S(1)}, u32[]{:S(2)}, u32[]{:S(2)}) collective-permute-start(bf16[768,768]{1,0:T(8,128)(2,1)S(1)} %get-tuple-element.139), channel_id=1, source_target_pairs={{0,1},{1,0},{2,3},{3,2},{4,5},{5,4},{6,7},{7,6},{8,9},{9,8},{10,11... | collective-permute-start | bytes 3538952 | tf_op jit(solution)/shard_map/ppermute | solution.py:903
  48.9 27.7 %collective-permute-start.11 = (bf16[2,384,768]{2,1,0:T(8,128)(2,1)S(1)}, bf16[2,384,768]{2,1,0:T(8,128)(2,1)S(1)}, u32[]{:S(2)}, u32[]{:S(2)}) collective-permute-start(bf16[2,384,768]{2,1,0:T(8,128)(2,1)S(1)} %get-tuple-element.161), channel_id=1, source_target_pairs={{0,4},{1,5},{2,6},{3,7},{4,0},{5,1},{6,2},{7,3},{8,12},{9,13},{10,... | collective-permute-start | bytes 3538952 | tf_op jit(solution)/shard_map/ppermute | solution.py:903
  51.4 19.1 %collective-permute-start.9 = (bf16[384,1024]{1,0:T(8,128)(2,1)S(1)}, bf16[384,1024]{1,0:T(8,128)(2,1)S(1)}, u32[]{:S(2)}, u32[]{:S(2)}) collective-permute-start(bf16[384,1024]{1,0:T(8,128)(2,1)S(1)} %get-tuple-element.146), channel_id=1, source_target_pairs={{0,8},{1,9},{2,10},{3,11},{4,12},{5,13},{6,14},{7,15},{8,0},{9,1},... | collective-permute-start | bytes 2359304 | tf_op jit(solution)/shard_map/ppermute | solution.py:903
  63.3 15.8 %collective-permute-start.12 = (bf16[256,3072]{1,0:T(8,128)(2,1)S(1)}, bf16[256,3072]{1,0:T(8,128)(2,1)S(1)}, u32[]{:S(2)}, u32[]{:S(2)}) collective-permute-start(bf16[256,3072]{1,0:T(8,128)(2,1)S(1)} %get-tuple-element.165.up_a), channel_id=1, source_target_pairs={{0,2},{1,3},{2,0},{3,1},{4,6},{5,7},{6,4},{7,5},{8,10},{9,11},{10,... | collective-permute-start | bytes 4718600 | tf_op jit(solution)/shard_map/ppermute | solution.py:903
  71.3 19.3 %collective-permute-start.13 = (bf16[192,1024]{1,0:T(8,128)(2,1)}, bf16[192,1024]{1,0:T(8,128)(2,1)}, u32[]{:S(2)}, u32[]{:S(2)}) collective-permute-start(bf16[192,1024]{1,0:T(8,128)(2,1)} %get-tuple-element.175), channel_id=1, source_target_pairs={{0,16},{1,17},{2,18},{3,19},{4,20},{5,21},{6,22},{7,23},{8,24},{9,... | collective-permute-start | bytes 1179656 | tf_op jit(solution)/shard_map/ppermute | solution.py:903
  76.9 16.0 %collective-permute-start.16 = (bf16[384,768]{1,0:T(8,128)(2,1)S(1)}, bf16[384,768]{1,0:T(8,128)(2,1)S(1)}, u32[]{:S(2)}, u32[]{:S(2)}) collective-permute-start(bf16[384,768]{1,0:T(8,128)(2,1)S(1)} %get-tuple-element.180), channel_id=1, source_target_pairs={{0,1},{1,0},{2,3},{3,2},{4,5},{5,4},{6,7},{7,6},{8,9},{9,8},{10,11... | collective-permute-start | bytes 1769480 | tf_op jit(solution)/shard_map/ppermute | solution.py:903
  77.6 15.3 %collective-permute-start.15 = (bf16[384,768]{1,0:T(8,128)(2,1)S(1)}, bf16[384,768]{1,0:T(8,128)(2,1)S(1)}, u32[]{:S(2)}, u32[]{:S(2)}) collective-permute-start(bf16[384,768]{1,0:T(8,128)(2,1)S(1)} %get-tuple-element.179), channel_id=1, source_target_pairs={{0,4},{1,5},{2,6},{3,7},{4,0},{5,1},{6,2},{7,3},{8,12},{9,13},{10,... | collective-permute-start | bytes 1769480 | tf_op jit(solution)/shard_map/ppermute | solution.py:903
  87.7 5.2 %collective-permute-start.14 = (f32[78,128]{1,0:T(8,128)S(1)}, f32[78,128]{1,0:T(8,128)S(1)}, u32[]{:S(2)}, u32[]{:S(2)}) collective-permute-start(f32[78,128]{1,0:T(8,128)S(1)} %pack.1), channel_id=1, source_target_pairs={{0,2},{1,3},{2,0},{3,1},{4,6},{5,7},{6,4},{7,5},{8,10},{9,11},{10,... | collective-permute-start | bytes 119816 | tf_op jit(solution)/shard_map/ppermute | solution.py:903
  91.8 13.2 %collective-permute-start.17 = (bf16[192,1152]{1,0:T(8,128)(2,1)S(1)}, bf16[192,1152]{1,0:T(8,128)(2,1)S(1)}, u32[]{:S(2)}, u32[]{:S(2)}) collective-permute-start(bf16[192,1152]{1,0:T(8,128)(2,1)S(1)} %copy-done.29), channel_id=1, source_target_pairs={{0,1},{1,0},{2,3},{3,2},{4,5},{5,4},{6,7},{7,6},{8,9},{9,8},{10,11... | collective-permute-start | bytes 1327112 | tf_op jit(solution)/shard_map/ppermute | solution.py:903
  92.4 13.1 %collective-permute-start.18 = (bf16[2,96,1152]{2,1,0:T(8,128)(2,1)S(1)}, bf16[2,96,1152]{2,1,0:T(8,128)(2,1)S(1)}, u32[]{:S(2)}, u32[]{:S(2)}) collective-permute-start(bf16[2,96,1152]{2,1,0:T(8,128)(2,1)S(1)} %copy-done.28), channel_id=1, source_target_pairs={{0,4},{1,5},{2,6},{3,7},{4,0},{5,1},{6,2},{7,3},{8,12},{9,13},{10,... | collective-permute-start | bytes 1327112 | tf_op jit(solution)/shard_map/ppermute | solution.py:903
  93.1 14.6 %collective-permute-start.19 = (bf16[192,1536]{1,0:T(8,128)(2,1)S(1)}, bf16[192,1536]{1,0:T(8,128)(2,1)S(1)}, u32[]{:S(2)}, u32[]{:S(2)}) collective-permute-start(bf16[192,1536]{1,0:T(8,128)(2,1)S(1)} %get-tuple-element.190), channel_id=1, source_target_pairs={{0,8},{1,9},{2,10},{3,11},{4,12},{5,13},{6,14},{7,15},{8,0},{9,1},... | collective-permute-start | bytes 1769480 | tf_op jit(solution)/shard_map/ppermute | solution.py:903
  93.9 20.5 %collective-permute-start.20 = (bf16[192,1152]{1,0:T(8,128)(2,1)S(1)}, bf16[192,1152]{1,0:T(8,128)(2,1)S(1)}, u32[]{:S(2)}, u32[]{:S(2)}) collective-permute-start(bf16[192,1152]{1,0:T(8,128)(2,1)S(1)} %copy-done.27), channel_id=1, source_target_pairs={{0,1},{1,0},{2,3},{3,2},{4,5},{5,4},{6,7},{7,6},{8,9},{9,8},{10,11... | collective-permute-start | bytes 1327112 | tf_op jit(solution)/shard_map/ppermute | solution.py:903
  95.4 19.6 %collective-permute-start.21 = (bf16[2,96,1152]{2,1,0:T(8,128)(2,1)S(1)}, bf16[2,96,1152]{2,1,0:T(8,128)(2,1)S(1)}, u32[]{:S(2)}, u32[]{:S(2)}) collective-permute-start(bf16[2,96,1152]{2,1,0:T(8,128)(2,1)S(1)} %copy-done.26), channel_id=1, source_target_pairs={{0,4},{1,5},{2,6},{3,7},{4,0},{5,1},{6,2},{7,3},{8,12},{9,13},{10,... | collective-permute-start | bytes 1327112 | tf_op jit(solution)/shard_map/ppermute | solution.py:903
  96.9 17.5 %copy-start.2 = (bf16[192,1152]{1,0:T(8,128)(2,1)S(1)}, bf16[192,1152]{1,0:T(8,128)(2,1)}, u32[]{:S(2)}) copy-start(bf16[192,1152]{1,0:T(8,128)(2,1)} %get-tuple-element.192.refs_0_) | copy-start | bytes 1327108
  105.6 13.6 %collective-permute-start.23 = (bf16[96,1152]{1,0:T(8,128)(2,1)S(1)}, bf16[96,1152]{1,0:T(8,128)(2,1)S(1)}, u32[]{:S(2)}, u32[]{:S(2)}) collective-permute-start(bf16[96,1152]{1,0:T(8,128)(2,1)S(1)} %get-tuple-element.203), channel_id=1, source_target_pairs={{0,1},{1,0},{2,3},{3,2},{4,5},{5,4},{6,7},{7,6},{8,9},{9,8},{10,11... | collective-permute-start | bytes 663560 | tf_op jit(solution)/shard_map/ppermute | solution.py:903
  107.1 12.5 %collective-permute-start.22 = (bf16[96,1152]{1,0:T(8,128)(2,1)S(1)}, bf16[96,1152]{1,0:T(8,128)(2,1)S(1)}, u32[]{:S(2)}, u32[]{:S(2)}) collective-permute-start(bf16[96,1152]{1,0:T(8,128)(2,1)S(1)} %get-tuple-element.202), channel_id=1, source_target_pairs={{0,4},{1,5},{2,6},{3,7},{4,0},{5,1},{6,2},{7,3},{8,12},{9,13},{10,... | collective-permute-start | bytes 663560 | tf_op jit(solution)/shard_map/ppermute | solution.py:903
  107.8 19.0 %collective-permute-start.27 = (bf16[96,1536]{1,0:T(8,128)(2,1)S(1)}, bf16[96,1536]{1,0:T(8,128)(2,1)S(1)}, u32[]{:S(2)}, u32[]{:S(2)}) collective-permute-start(bf16[96,1536]{1,0:T(8,128)(2,1)S(1)} %get-tuple-element.213), channel_id=1, source_target_pairs={{0,16},{1,17},{2,18},{3,19},{4,20},{5,21},{6,22},{7,23},{8,24},{9,... | collective-permute-start | bytes 884744 | tf_op jit(solution)/shard_map/ppermute | solution.py:903
  115.1 7.2 %collective-permute-start.25 = (bf16[96,1152]{1,0:T(8,128)(2,1)S(1)}, bf16[96,1152]{1,0:T(8,128)(2,1)S(1)}, u32[]{:S(2)}, u32[]{:S(2)}) collective-permute-start(bf16[96,1152]{1,0:T(8,128)(2,1)S(1)} %get-tuple-element.207), channel_id=1, source_target_pairs={{0,1},{1,0},{2,3},{3,2},{4,5},{5,4},{6,7},{7,6},{8,9},{9,8},{10,11... | collective-permute-start | bytes 663560 | tf_op jit(solution)/shard_map/ppermute | solution.py:903
  116.6 6.5 %collective-permute-start.24 = (bf16[96,1152]{1,0:T(8,128)(2,1)S(1)}, bf16[96,1152]{1,0:T(8,128)(2,1)S(1)}, u32[]{:S(2)}, u32[]{:S(2)}) collective-permute-start(bf16[96,1152]{1,0:T(8,128)(2,1)S(1)} %get-tuple-element.206), channel_id=1, source_target_pairs={{0,4},{1,5},{2,6},{3,7},{4,0},{5,1},{6,2},{7,3},{8,12},{9,13},{10,... | collective-permute-start | bytes 663560 | tf_op jit(solution)/shard_map/ppermute | solution.py:903
  119.8 8.4 %collective-permute-start.28 = (bf16[48,2304]{1,0:T(8,128)(2,1)S(1)}, bf16[48,2304]{1,0:T(8,128)(2,1)S(1)}, u32[]{:S(2)}, u32[]{:S(2)}) collective-permute-start(bf16[48,2304]{1,0:T(8,128)(2,1)S(1)} %get-tuple-element.210), channel_id=1, source_target_pairs={{0,8},{1,9},{2,10},{3,11},{4,12},{5,13},{6,14},{7,15},{8,0},{9,1},... | collective-permute-start | bytes 663560 | tf_op jit(solution)/shard_map/ppermute | solution.py:903
  120.5 4.5 %collective-permute-start.26 = (f32[78,128]{1,0:T(8,128)S(1)}, f32[78,128]{1,0:T(8,128)S(1)}, u32[]{:S(2)}, u32[]{:S(2)}) collective-permute-start(f32[78,128]{1,0:T(8,128)S(1)} %add.39), channel_id=1, source_target_pairs={{0,1},{1,0},{2,3},{3,2},{4,5},{5,4},{6,7},{7,6},{8,9},{9,8},{10,11... | collective-permute-start | bytes 119816 | tf_op jit(solution)/shard_map/ppermute | solution.py:903
  122.2 6.1 %collective-permute-start.29 = (bf16[96,1024]{1,0:T(8,128)(2,1)S(1)}, bf16[96,1024]{1,0:T(8,128)(2,1)S(1)}, u32[]{:S(2)}, u32[]{:S(2)}) collective-permute-start(bf16[96,1024]{1,0:T(8,128)(2,1)S(1)} %get-tuple-element.217), channel_id=1, source_target_pairs={{0,1},{1,0},{2,3},{3,2},{4,5},{5,4},{6,7},{7,6},{8,9},{9,8},{10,11... | collective-permute-start | bytes 589832 | tf_op jit(solution)/shard_map/ppermute | solution.py:903
  125.0 4.0 %collective-permute-start.30 = (f32[78,128]{1,0:T(8,128)S(1)}, f32[78,128]{1,0:T(8,128)S(1)}, u32[]{:S(2)}, u32[]{:S(2)}) collective-permute-start(f32[78,128]{1,0:T(8,128)S(1)} %add.40), channel_id=1, source_target_pairs={{0,4},{1,5},{2,6},{3,7},{4,0},{5,1},{6,2},{7,3},{8,12},{9,13},{10,... | collective-permute-start | bytes 119816 | tf_op jit(solution)/shard_map/ppermute | solution.py:903
  125.5 10.9 %collective-permute-start.32 = (bf16[48,2304]{1,0:T(8,128)(2,1)S(1)}, bf16[48,2304]{1,0:T(8,128)(2,1)S(1)}, u32[]{:S(2)}, u32[]{:S(2)}) collective-permute-start(bf16[48,2304]{1,0:T(8,128)(2,1)S(1)} %get-tuple-element.222), channel_id=1, source_target_pairs={{0,8},{1,9},{2,10},{3,11},{4,12},{5,13},{6,14},{7,15},{8,0},{9,1},... | collective-permute-start | bytes 663560 | tf_op jit(solution)/shard_map/ppermute | solution.py:903
  129.0 4.9 %collective-permute-start.31 = (f32[78,128]{1,0:T(8,128)S(1)}, f32[78,128]{1,0:T(8,128)S(1)}, u32[]{:S(2)}, u32[]{:S(2)}) collective-permute-start(f32[78,128]{1,0:T(8,128)S(1)} %add.42), channel_id=1, source_target_pairs={{0,8},{1,9},{2,10},{3,11},{4,12},{5,13},{6,14},{7,15},{8,0},{9,1},... | collective-permute-start | bytes 119816 | tf_op jit(solution)/shard_map/ppermute | solution.py:903
  130.4 6.1 %collective-permute-start.33 = (bf16[48,1024]{1,0:T(8,128)(2,1)S(1)}, bf16[48,1024]{1,0:T(8,128)(2,1)S(1)}, u32[]{:S(2)}, u32[]{:S(2)}) collective-permute-start(bf16[48,1024]{1,0:T(8,128)(2,1)S(1)} %get-tuple-element.224), channel_id=1, source_target_pairs={{0,4},{1,5},{2,6},{3,7},{4,0},{5,1},{6,2},{7,3},{8,12},{9,13},{10,... | collective-permute-start | bytes 294920 | tf_op jit(solution)/shard_map/ppermute | solution.py:903
  130.8 8.5 %collective-permute-start.34 = (bf16[24,2304]{1,0:T(8,128)(2,1)S(1)}, bf16[24,2304]{1,0:T(8,128)(2,1)S(1)}, u32[]{:S(2)}, u32[]{:S(2)}) collective-permute-start(bf16[24,2304]{1,0:T(8,128)(2,1)S(1)} %slice.122), channel_id=1, source_target_pairs={{0,16},{1,17},{2,18},{3,19},{4,20},{5,21},{6,22},{7,23},{8,24},{9,... | collective-permute-start | bytes 331784 | tf_op jit(solution)/shard_map/ppermute | solution.py:903
  133.9 6.4 %collective-permute-start.35 = (f32[78,128]{1,0:T(8,128)S(1)}, f32[78,128]{1,0:T(8,128)S(1)}, u32[]{:S(2)}, u32[]{:S(2)}) collective-permute-start(f32[78,128]{1,0:T(8,128)S(1)} %add.43), channel_id=1, source_target_pairs={{0,16},{1,17},{2,18},{3,19},{4,20},{5,21},{6,22},{7,23},{8,24},{9,... | collective-permute-start | bytes 119816 | tf_op jit(solution)/shard_map/ppermute | solution.py:903
  140.3 7.6 %collective-permute-start.36 = (bf16[24,2304]{1,0:T(8,128)(2,1)S(1)}, bf16[24,2304]{1,0:T(8,128)(2,1)S(1)}, u32[]{:S(2)}, u32[]{:S(2)}) collective-permute-start(bf16[24,2304]{1,0:T(8,128)(2,1)S(1)} %slice.121), channel_id=1, source_target_pairs={{0,16},{1,17},{2,18},{3,19},{4,20},{5,21},{6,22},{7,23},{8,24},{9,... | collective-permute-start | bytes 331784 | tf_op jit(solution)/shard_map/ppermute | solution.py:903
  (19 other events, 178.6 us)
